TPU v7x, 32 devices: a whole 2x2x4 slice. The times are simulated.
32 devices in a mesh: gx: 4 (over z), gy: 8 (over y, x, core).
Axes of the slice: x: 2, y: 2, z: 4, core: 2. Of those that a mesh axis runs over, the one named last changes fastest.
Arguments:
- movie: bfloat16 [32, 64, 128, 128], P('gx', 'gy'), may hold values from -14 to 14
- brain_mask: int32 [32, 64, 128], P('gx', 'gy'), may hold values 0 or 1
Outputs:
- fitted: bfloat16 [32, 64, 128, 128], P('gx', 'gy')
- propagator: float32 [127, 127], replicated
All inputs are finite; a program needn't handle non-finite values. No bound on the sum of `brain_mask` on one device may be relied on, other than what follows from the above.
Results may differ from a plain program's by a relative error of at most 0.00095.
Values may be sent and summed in bfloat16 or wider, within the bound.
A program may use at most 128 MiB of HBM per device.

v0:
```python
import jax
import jax.numpy as jnp
from jax import lax
from jax.sharding import PartitionSpec as P

RAD = 4


def extended(x, sides, width):
    for axis, dim in sides:
        peers, length = (lax.axis_size(axis), x.shape[dim])
        up = [(i, (i + 1) % peers) for i in range(peers - 1)]
        down = [(j, i) for i, j in up]
        last = lax.slice_in_dim(x, length - width, length, axis=dim)
        initial = lax.slice_in_dim(x, 0, width, axis=dim)
        before = lax.ppermute(last, axis, up)
        after = lax.ppermute(initial, axis, down)
        x = jnp.concatenate([before, x, after], axis=dim)
    return x


def kernel_weights():
    offsets = jnp.arange(-RAD, RAD + 1).astype(jnp.float32)
    sigma = RAD / 2.0
    raw = jnp.exp(-offsets * offsets / (2.0 * sigma * sigma))
    return raw / jnp.sum(raw)


def taps_along(field, axis, weights, length):
    total = jnp.zeros(field.shape[:axis] + (length,) + field.shape[axis + 1 :], jnp.float32)
    for k in range(2 * RAD + 1):
        total = total + weights[k] * lax.slice_in_dim(field, k, k + length, axis=axis)
    return total


def chol_solve(factor, right):
    middle = lax.linalg.triangular_solve(factor, right, left_side=True, lower=True)
    return lax.linalg.triangular_solve(factor, middle, left_side=True, lower=True, transpose_a=True)


def on_device(movie, brain_mask):
    size_x, size_y, size_z, frames = movie.shape
    weights = kernel_weights()
    padded = extended(movie, (("gx", 0), ("gy", 1)), RAD)
    wide = jnp.pad(padded.astype(jnp.float32), ((0, 0), (0, 0), (RAD, RAD), (0, 0)))
    blur = taps_along(wide, 2, weights, size_z)
    blur = taps_along(blur, 1, weights, size_y)
    blur = taps_along(blur, 0, weights, size_x)
    mask_f = brain_mask.astype(jnp.float32)[:, :, :, None]
    filtered = (mask_f * (movie.astype(jnp.float32) - blur)).reshape(-1, frames)
    local_gram = lax.dot_general(
        filtered,
        filtered,
        (((0,), (0,)), ((), ())),
        precision=lax.Precision.HIGHEST,
        preferred_element_type=jnp.float32,
    )
    gram = lax.psum(local_gram, ("gx", "gy"))
    g_left = gram[: frames - 1, : frames - 1]
    g_right = gram[: frames - 1, 1:]
    lam = 0.5 * jnp.trace(g_left) / (frames - 1)
    factor = jnp.linalg.cholesky(g_left + lam * jnp.eye(frames - 1, dtype=jnp.float32))
    propagator = chol_solve(factor, g_right)
    advance = jnp.zeros((frames, frames), jnp.float32)
    advance = advance.at[0, 0].set(1.0)
    advance = advance.at[: frames - 1, 1:].set(propagator)
    fitted = jnp.dot(
        filtered, advance, precision=lax.Precision.HIGHEST, preferred_element_type=jnp.float32
    )
    fitted = fitted.astype(jnp.bfloat16).reshape(size_x, size_y, size_z, frames)
    return (fitted, propagator)


def solution(mesh):
    return jax.shard_map(
        on_device,
        mesh=mesh,
        in_specs=(P("gx", "gy", None, None), P("gx", "gy", None)),
        out_specs=(P("gx", "gy", None, None), P()),
        check_vma=False,
    )
```

profile of v0, /device:TPU:0, one launch (start us, length us, event | category | flops | bytes accessed | tf_op | source)
XLA Modules:
  0.0 387.9 jit_solution(6324855753055116150)
XLA Ops:
  7.2 1.7 fusion.34
  8.9 5.0 %collective-permute-start = (bf16[4,8,128,128]{3,2,1,0:T(8,128)(2,1)S(1)}, bf16[4,8,128,128]{3,2,1,0:T(8,128)(2,1)S(1)}, u32[]{:S(2)}, u32[]{:S(2)}) collective-permute-start(bf16[4,8,128,128]{3,2,1,0:T(8,128)(2,1)S(1)} %get-tuple-element.29), channel_id=1, source_target_pairs={{0,8},{8,16},{16,24},{1,9},{9,17},{17,25},{2,10},{10,18},{18,26},{... | collective-permute-start | bytes 3145736 | tf_op jit(solution)/shard_map/ppermute | solution.py:16
  13.9 1.3 collective-permute-start.1
  15.2 21.0 %collective-permute-done = bf16[4,8,128,128]{3,2,1,0:T(8,128)(2,1)S(1)} collective-permute-done((bf16[4,8,128,128]{3,2,1,0:T(8,128)(2,1)S(1)}, bf16[4,8,128,128]{3,2,1,0:T(8,128)(2,1)S(1)}, u32[]{:S(2)}, u32[]{:S(2)}) %collective-permute-start) | collective-permute-done | bytes 1048608 | tf_op jit(solution)/shard_map/ppermute | solution.py:16
  36.3 2.0 constant_dynamic-update-slice_fusion.1
  38.3 2.1 collective-permute-done.1
  41.1 1.4 collective-permute-start.2
  42.6 1.3 collective-permute-start.3
  46.2 4.0 %collective-permute-done.3 = bf16[16,4,128,128]{3,2,1,0:T(8,128)(2,1)S(1)} collective-permute-done((bf16[16,4,128,128]{3,2,1,0:T(8,128)(2,1)S(1)}, bf16[16,4,128,128]{3,2,1,0:T(8,128)(2,1)S(1)}, u32[]{:S(2)}, u32[]{:S(2)}) %collective-permute-start.3) | collective-permute-done | bytes 2097184 | tf_op jit(solution)/shard_map/ppermute | solution.py:17
  50.2 6.0 %maximum_convert_fusion = f32[16,16,128,128]{3,2,1,0:T(8,128)} fusion(bf16[16,4,128,128]{3,2,1,0:T(8,128)(2,1)S(1)} %collective-permute-done.3, bf16[16,8,128,128]{3,2,1,0:T(8,128)(2,1)S(1)} %constant_dynamic-update-slice_fusion, bf16[16,4,128,128]{3,2,1,0:T(8,128)(2,1)S(1)} %collective-permute-done.2), kind=kLoop, calls=%fused_computation.27 | loop fusion | flops 12582912 | bytes 25165824 | tf_op jit(solution)/shard_map/convert_element_type | solution.py:45
  56.2 74.3 %multiply_add_fusion = f32[16,16,128,128]{3,2,1,0:T(8,128)} fusion(f32[16,16,128,128]{3,2,1,0:T(8,128)} %maximum_convert_fusion, f32[]{:T(128)} %bitcast.8, f32[]{:T(128)} %bitcast.7, f32[]{:T(128)} %bitcast.6, f32[]{:T(128)} %bitcast.5, f32[]{:T(128)} %bitcast.4, f32[]{:T(128)} %bitcast.3, f32[]{:T(128)} %bitcast.2, f32[]{:T(128)} %bitcast.1, f32[]{:T(128)} %bitcast), kind=kLoop, calls=%fused_computation | loop fusion | flops 71303168 | bytes 33554468 | tf_op jit(solution)/shard_map/add | solution.py:32
  130.5 33.2 %fusion.5 = f32[16,8,128,128]{3,2,1,0:T(8,128)S(1)} fusion(f32[16,16,128,128]{3,2,1,0:T(8,128)} %multiply_add_fusion, f32[]{:T(128)} %bitcast.8, f32[]{:T(128)} %bitcast.7, f32[]{:T(128)} %bitcast.6, f32[]{:T(128)} %bitcast.5, f32[]{:T(128)} %bitcast.4, f32[]{:T(128)} %bitcast.3, f32[]{:T(128)} %bitcast.2, f32[]{:T(128)} %bitcast.1, f32[]{:T(128)} %bitcast), kind=kLoop, calls=%fused_computation.11 | loop fusion | flops 35651584 | bytes 83886112 | tf_op jit(solution)/shard_map/add | solution.py:32
  163.7 10.5 %fusion.15 = f32[8,8,128,128]{3,2,1,0:T(8,128)S(1)} fusion(f32[16,8,128,128]{3,2,1,0:T(8,128)S(1)} %fusion.5, bf16[8,8,128,128]{3,2,1,0:T(8,128)(2,1)S(1)} %copy-done.1, f32[]{:T(128)} %bitcast.8, f32[]{:T(128)} %bitcast.7, f32[]{:T(128)} %bitcast.6, f32[]{:T(128)} %bitcast.5, f32[]{:T(128)} %bitcast.4, f32[]{:T(128)} %bitcast.3, f32[]{:T(128)} %bitcast.2, ...), kind=kLoop, calls=%fused_computation.31 | loop fusion | flops 20971520 | bytes 44072996 | tf_op jit(solution)/shard_map/mul | solution.py:50
  174.2 1.9 copy-done
  176.2 7.6 %convolution_bitcast_fusion = f32[128,128]{1,0:T(8,128)} fusion(f32[8,8,128,128]{3,2,1,0:T(8,128)S(1)} %fusion.15), kind=kOutput, calls=%fused_computation.47 | convolution fusion | flops 1610612736 | bytes 4259840 | tf_op jit(solution)/shard_map/dot_general | solution.py:51
  185.0 156.8 %all-reduce.3.cloned.1.call-done = f32[128,128]{1,0:T(8,128)} async-done(((f32[128,128]{1,0:T(8,128)}), f32[128,128]{1,0:T(8,128)}) %all-reduce.3.cloned.1.call-update) | async-done | bytes 65552 | tf_op jit(solution)/shard_map/psum | solution.py:58
  341.9 1.5 select_reduce_fusion.1
  344.9 0.9 fusion.29
  345.8 11.6 %cholesky.17 = f32[127,127]{1,0:T(8,128)S(1)} custom-call(f32[127,127]{1,0:T(8,128)S(1)} %fusion.29), custom_call_target="Cholesky" | custom-call | tf_op jit(solution)/shard_map/jit(cholesky)/cholesky | solution.py:62
  358.8 9.7 %custom-call.8 = f32[1,127,127]{1,2,0:T(8,128)S(1)} custom-call(f32[1,127,127]{2,1,0:T(8,128)S(1)} %fusion.23), custom_call_target="InvertDiagBlocksLowerTriangular" | custom-call | tf_op jit(solution)/shard_map/triangular_solve | solution.py:38
  368.5 1.2 fusion.24
  369.7 2.7 dynamic-slice_select_fusion
  372.4 2.5 scatter.4
  374.9 6.2 %convolution_convert_fusion = bf16[8192,128]{1,0:T(8,128)(2,1)} fusion(f32[8192,128]{1,0:T(8,128)} %bitcast.35, f32[128,128]{1,0:T(8,128)S(1)} %scatter.4), kind=kOutput, calls=%fused_computation.9 | convolution fusion | flops 1611661312 | bytes 6356992 | tf_op jit(solution)/shard_map/dot_general | solution.py:67
  (26 shorter events, 6.8 us)
Async XLA Ops:
  7.2 334.7 %all-reduce.3.cloned.1.call-start = ((), (), s32[]{:S(2)}) async-start(), calls=%async_computation | async-start | bytes 131072 | tf_op jit(solution)/shard_map/psum | solution.py:58
  8.9 27.3 %collective-permute-start = (bf16[4,8,128,128]{3,2,1,0:T(8,128)(2,1)S(1)}, bf16[4,8,128,128]{3,2,1,0:T(8,128)(2,1)S(1)}, u32[]{:S(2)}, u32[]{:S(2)}) collective-permute-start(bf16[4,8,128,128]{3,2,1,0:T(8,128)(2,1)S(1)} %get-tuple-element.29), channel_id=1, source_target_pairs={{0,8},{8,16},{16,24},{1,9},{9,17},{17,25},{2,10},{10,18},{18,26},{... | collective-permute-start | bytes 3145736 | tf_op jit(solution)/shard_map/ppermute | solution.py:16
  13.9 30.0 %copy-start.3 = (s32[8,8,128]{2,1,0:T(8,128)S(1)}, s32[8,8,128]{2,1,0:T(8,128)}, u32[]{:S(2)}) copy-start(s32[8,8,128]{2,1,0:T(8,128)} %param.7) | copy-start | bytes 98308
  13.9 26.5 %collective-permute-start.1 = (bf16[4,8,128,128]{3,2,1,0:T(8,128)(2,1)S(1)}, bf16[4,8,128,128]{3,2,1,0:T(8,128)(2,1)S(1)}, u32[]{:S(2)}, u32[]{:S(2)}) collective-permute-start(bf16[4,8,128,128]{3,2,1,0:T(8,128)(2,1)S(1)} %get-tuple-element.28), channel_id=1, source_target_pairs={{8,0},{16,8},{24,16},{9,1},{17,9},{25,17},{10,2},{18,10},{26,18},{... | collective-permute-start | bytes 3145736 | tf_op jit(solution)/shard_map/ppermute | solution.py:17
  41.1 5.1 %collective-permute-start.2 = (bf16[16,4,128,128]{3,2,1,0:T(8,128)(2,1)S(1)}, bf16[16,4,128,128]{3,2,1,0:T(8,128)(2,1)S(1)}, u32[]{:S(2)}, u32[]{:S(2)}) collective-permute-start(bf16[16,4,128,128]{3,2,1,0:T(8,128)(2,1)S(1)} %get-tuple-element.26), channel_id=1, source_target_pairs={{0,1},{1,2},{2,3},{3,4},{4,5},{5,6},{6,7},{8,9},{9,10},{10,11},{11... | collective-permute-start | bytes 6291464 | tf_op jit(solution)/shard_map/ppermute | solution.py:16
  42.6 7.6 %collective-permute-start.3 = (bf16[16,4,128,128]{3,2,1,0:T(8,128)(2,1)S(1)}, bf16[16,4,128,128]{3,2,1,0:T(8,128)(2,1)S(1)}, u32[]{:S(2)}, u32[]{:S(2)}) collective-permute-start(bf16[16,4,128,128]{3,2,1,0:T(8,128)(2,1)S(1)} %get-tuple-element.27), channel_id=1, source_target_pairs={{1,0},{2,1},{3,2},{4,3},{5,4},{6,5},{7,6},{9,8},{10,9},{11,10},{12... | collective-permute-start | bytes 6291464 | tf_op jit(solution)/shard_map/ppermute | solution.py:17
  130.5 33.2 %copy-start.1 = (bf16[8,8,128,128]{3,2,1,0:T(8,128)(2,1)S(1)}, bf16[8,8,128,128]{3,2,1,0:T(8,128)(2,1)}, u32[]{:S(2)}) copy-start(bf16[8,8,128,128]{3,2,1,0:T(8,128)(2,1)} %param.6) | copy-start | bytes 6291460
  174.2 1.9 copy-start
  176.2 8.9 %copy-start.2 = (f32[128,128]{1,0:T(8,128)S(1)}, f32[128,128]{1,0:T(8,128)}, u32[]{:S(2)}) copy-start(f32[128,128]{1,0:T(8,128)} %constant.113.clone.1) | copy-start | bytes 196612
Sparse Core Ops, SparseCore 0:
  183.9 157.9 all-reduce.2
where the time goes:
time: 390 us; the launch traced here: 388 us
  waiting for transfers between devices  184 us (47%)
  other arithmetic  152 us (39%)
  matrix products  17.6 us (5%)
  between operations  14.9 us (4%)
  local copies, waits for them, and re-layouts  10.2 us (3%)
  starting transfers between devices  9.04 us (2%)
    psum x1, waiting for transfers between devices, on_device(): gram = lax.psum(local_gram, ('gx', 'gy'))  157 us
    add x2, other arithmetic, taps_along(): total + weights[k] * lax.slice_in_dim(field, k, k + length, axis=axis)  107 us
    ppermute x2, waiting for transfers between devices, extended(): before = lax.ppermute(last, axis, up)  21.4 us
    another operation x3, other arithmetic, on_device(): jnp.linalg.cholesky(g_left + lam * jnp.eye(frames - 1, dtype=jnp.float32))  12.3 us
    mul x1, other arithmetic, on_device(): filtered = (mask_f * (movie.astype(jnp.float32) - blur)).reshape(-1, frames)  10.5 us
    another operation x2, other arithmetic, chol_solve(): lax.linalg.triangular_solve(factor, middle, left_side=True, lower=True, t...  10.4 us
  transfers between devices with their start and end apart: 5, of which 5 were waited for; matrix products, arithmetic and copies ran while one was open for 1% of the time, Pallas kernels for 0%

commit v1 on v0

v1 whole, which is shorter than its diff:
```python
import functools

import numpy as np
import jax
import jax.numpy as jnp
from jax import lax
from jax.experimental import pallas as pl
from jax.experimental.pallas import tpu as pltpu
from jax.sharding import PartitionSpec as P

RAD = 4
MESH = pl.DeviceIdType.MESH
F32 = jnp.float32
BF16 = jnp.bfloat16


def weights():
    k = np.arange(-RAD, RAD + 1).astype(np.float32)
    sigma = RAD / 2.0
    raw = np.exp(-k * k / np.float32(2.0 * sigma * sigma)).astype(np.float32)
    w = raw / raw.sum(dtype=np.float32)
    return [float(w[RAD + j]) for j in range(RAD + 1)]


W = weights()


def blur9(items, at):
    total = W[0] * items[at + RAD]
    for k in range(1, RAD + 1):
        total = total + W[k] * (items[at + RAD - k] + items[at + RAD + k])
    return total


def split(v):
    hi = v.astype(BF16)
    return hi, (v - hi.astype(F32)).astype(BF16)


def filter_kernel(
    nx, ny,
    movie, mask, filt, gram_out,
    ylo, yhi, ysend, xlo, xhi, yb, xb, band, maskt, gacc, gpart, rsbuf, xbuf, gfull,
    ysl, ysh, yrl, yrh, xsl, xsh, xrl, xrh, s1, r1, s2, r2, s3, r3,
):
    cx, cy, cz, fr = movie.shape
    gx, gy = lax.axis_index("gx"), lax.axis_index("gy")
    barrier = pltpu.get_barrier_semaphore()

    def hello_y(d, c):
        pl.semaphore_signal(barrier, inc=1, device_id=(gx, lax.rem(gy + d, ny)), device_id_type=MESH)
        return c

    def hello_x(d, c):
        pl.semaphore_signal(barrier, inc=1, device_id=(lax.rem(gx + d, nx), gy), device_id_type=MESH)
        return c

    lax.fori_loop(1, ny, hello_y, 0)
    lax.fori_loop(1, nx, hello_x, 0)
    pl.semaphore_wait(barrier, ny - 1 + nx - 1)

    has_yl, has_yh = gy > 0, gy < ny - 1
    has_xl, has_xh = gx > 0, gx < nx - 1

    def order(i):
        return jnp.where(i % 2 == 0, i // 2, cx - 1 - i // 2)

    def y_up(l):
        return pltpu.make_async_remote_copy(
            src_ref=movie.at[l, pl.ds(cy - RAD, RAD)], dst_ref=ylo.at[l],
            send_sem=ysl.at[l], recv_sem=yrl.at[l],
            device_id=(gx, gy + 1), device_id_type=MESH)

    def y_down(l):
        return pltpu.make_async_remote_copy(
            src_ref=movie.at[l, pl.ds(0, RAD)], dst_ref=yhi.at[l],
            send_sem=ysh.at[l], recv_sem=yrh.at[l],
            device_id=(gx, gy - 1), device_id_type=MESH)

    def x_up(j):
        return pltpu.make_async_remote_copy(
            src_ref=ysend.at[cx - RAD + j], dst_ref=xlo.at[j],
            send_sem=xsl.at[j], recv_sem=xrl.at[j],
            device_id=(gx + 1, gy), device_id_type=MESH)

    def x_down(j):
        return pltpu.make_async_remote_copy(
            src_ref=ysend.at[j], dst_ref=xhi.at[j],
            send_sem=xsh.at[j], recv_sem=xrh.at[j],
            device_id=(gx - 1, gy), device_id_type=MESH)

    def start_y(i, c):
        l = order(i)

        @pl.when(has_yh)
        def _():
            y_up(l).start()

        @pl.when(has_yl)
        def _():
            y_down(l).start()
        return c

    lax.fori_loop(0, cx, start_y, 0)

    @pl.when(jnp.logical_not(has_yl))
    def _():
        ylo[...] = jnp.zeros_like(ylo)

    @pl.when(jnp.logical_not(has_yh))
    def _():
        yhi[...] = jnp.zeros_like(yhi)

    @pl.when(jnp.logical_not(has_xl))
    def _():
        xlo[...] = jnp.zeros_like(xlo)

    @pl.when(jnp.logical_not(has_xh))
    def _():
        xhi[...] = jnp.zeros_like(xhi)

    dist = jnp.abs(lax.broadcasted_iota(jnp.int32, (cz, cz), 0) - lax.broadcasted_iota(jnp.int32, (cz, cz), 1))
    t = jnp.zeros((cz, cz), F32)
    for k in range(RAD + 1):
        t = jnp.where(dist == k, W[k], t)
    th, tl = split(t)
    band[:, 0:cz] = th
    band[:, cz:2 * cz] = tl
    band[:, 2 * cz:3 * cz] = th
    maskt[...] = jnp.transpose(mask[...].astype(F32).reshape(cx * cy, cz)).astype(BF16)
    gacc[...] = jnp.zeros_like(gacc)

    ZT = 16

    def y_layer(i, c):
        l = order(i)

        @pl.when(has_yl)
        def _():
            y_up(l).wait_recv()

        @pl.when(has_yh)
        def _():
            y_down(l).wait_recv()

        def tile(z, c2):
            rows = pl.ds(pl.multiple_of(z * ZT, ZT), ZT)
            items = [ylo[l, k, rows, :].astype(F32) for k in range(RAD)]
            items += [movie[l, k, rows, :].astype(F32) for k in range(cy)]
            items += [yhi[l, k, rows, :].astype(F32) for k in range(RAD)]
            for y in range(cy):
                v = blur9(items, y)
                yb[l + RAD, y, rows, :] = v
                ysend[l, y, rows, :] = v.astype(BF16)
            return c2

        lax.fori_loop(0, cz // ZT, tile, 0)

        @pl.when(jnp.logical_and(i % 2 == 0, has_xl))
        def _():
            x_down(i // 2).start()

        @pl.when(jnp.logical_and(i % 2 == 1, has_xh))
        def _():
            x_up(RAD - 1 - i // 2).start()
        return c

    lax.fori_loop(0, cx, y_layer, 0)

    def widen(src, j, to):
        def tile(z, c):
            rows = pl.ds(pl.multiple_of(z * ZT, ZT), ZT)
            for y in range(cy):
                yb[to, y, rows, :] = src[j, y, rows, :].astype(F32)
            return c
        lax.fori_loop(0, cz // ZT, tile, 0)

    def x_layer(l):
        def tile(z, c):
            rows = pl.ds(pl.multiple_of(z * ZT, ZT), ZT)
            for y in range(cy):
                items = [yb[l + k, y, rows, :] for k in range(2 * RAD + 1)]
                xb[y, rows, :] = blur9(items, 0)
            return c
        lax.fori_loop(0, cz // ZT, tile, 0)
        lanes = lax.broadcasted_iota(jnp.int32, (cx * cy, fr), 0)
        for y in range(0, cy, 2):
            parts = [split(xb[y + k]) for k in range(2)]
            hi = jnp.concatenate([p[0] for p in parts], axis=1)
            lo = jnp.concatenate([p[1] for p in parts], axis=1)
            blur = jnp.dot(band[...], jnp.concatenate([hi, hi, lo], axis=0), preferred_element_type=F32)
            left, right = [], []
            for k in range(2):
                one = jnp.where(lanes == l * cy + y + k, 1.0, 0.0).astype(BF16)
                m = jnp.dot(maskt[...], one, preferred_element_type=F32)
                f = m * (movie[l, y + k].astype(F32) - blur[:, k * fr:(k + 1) * fr])
                fh, fl = split(f)
                both = jnp.concatenate([fh, fl], axis=1)
                filt[l, y + k] = both
                left.append(fh)
                right.append(both)
            gacc[...] += lax.dot_general(
                jnp.concatenate(left, axis=0), jnp.concatenate(right, axis=0),
                (((0,), (0,)), ((), ())), preferred_element_type=F32)

    def x_step(j, c):
        @pl.when(has_xl)
        def _():
            x_up(RAD - 1 - j).wait_recv()

        @pl.when(has_xh)
        def _():
            x_down(j).wait_recv()
        widen(xlo, RAD - 1 - j, RAD - 1 - j)
        widen(xhi, j, cx + RAD + j)

        def two(s, c2):
            x_layer(jnp.where(s == 0, RAD - 1 - j, cx - RAD + j))
            return c2
        lax.fori_loop(0, 2, two, 0)
        return c

    lax.fori_loop(0, RAD, x_step, 0)

    g = gacc[:, 0:fr] + gacc[:, fr:2 * fr] + jnp.transpose(gacc[:, fr:2 * fr])
    r = fr // ny
    for p in range(ny):
        gpart[p] = g[p * r:(p + 1) * r]

    def scatter(d):
        to = lax.rem(gy + d, ny)
        return pltpu.make_async_remote_copy(
            src_ref=gpart.at[to], dst_ref=rsbuf.at[d], send_sem=s1.at[d], recv_sem=r1.at[d],
            device_id=(gx, to), device_id_type=MESH)

    def across(d):
        return pltpu.make_async_remote_copy(
            src_ref=xbuf.at[gx], dst_ref=xbuf.at[gx], send_sem=s2.at[d], recv_sem=r2.at[d],
            device_id=(lax.rem(gx + d, nx), gy), device_id_type=MESH)

    def gather(d):
        return pltpu.make_async_remote_copy(
            src_ref=gfull.at[gy], dst_ref=gfull.at[gy], send_sem=s3.at[d], recv_sem=r3.at[d],
            device_id=(gx, lax.rem(gy + d, ny)), device_id_type=MESH)

    def each(n, f):
        def body(d, c):
            f(d)
            return c
        lax.fori_loop(1, n, body, 0)

    each(ny, lambda d: scatter(d).start())
    each(ny, lambda d: scatter(d).wait_recv())
    total = gpart[gy]
    for d in range(1, ny):
        total = total + rsbuf[d]
    xbuf[gx] = total
    each(nx, lambda d: across(d).start())
    each(nx, lambda d: across(d).wait_recv())
    total = xbuf[0]
    for d in range(1, nx):
        total = total + xbuf[d]
    gfull[gy] = total
    each(ny, lambda d: gather(d).start())
    each(ny, lambda d: gather(d).wait_recv())
    gram_out[...] = gfull[...]

    each(ny, lambda d: scatter(d).wait_send())
    each(nx, lambda d: across(d).wait_send())
    each(ny, lambda d: gather(d).wait_send())

    def drain_y(l, c):
        @pl.when(has_yh)
        def _():
            y_up(l).wait_send()

        @pl.when(has_yl)
        def _():
            y_down(l).wait_send()
        return c

    def drain_x(j, c):
        @pl.when(has_xh)
        def _():
            x_up(j).wait_send()

        @pl.when(has_xl)
        def _():
            x_down(j).wait_send()
        return c

    lax.fori_loop(0, cx, drain_y, 0)
    lax.fori_loop(0, RAD, drain_x, 0)


def fit_kernel(gram, filt, out, prop, a, b, m):
    fr = gram.shape[0]

    @pl.when(pl.program_id(0) == 0)
    def _():
        g = gram[...]
        row = lax.broadcasted_iota(jnp.int32, (fr, fr), 0)
        col = lax.broadcasted_iota(jnp.int32, (fr, fr), 1)
        diag = jnp.where((row == col) & (row < fr - 1), g, 0.0)
        lam = 0.5 * jnp.sum(diag) / (fr - 1)
        last = (row == fr - 1) | (col == fr - 1)
        a[...] = jnp.where(last, 0.0, g) + jnp.where(row == col, lam, 0.0)
        b[...] = jnp.where(row == fr - 1, 0.0, g)

        def block(i, c):
            group = pl.ds(pl.multiple_of(i * 8, 8), 8)
            sub = lax.broadcasted_iota(jnp.int32, (8, fr), 0)
            for s in range(0, 8, 2):
                ga, gb = a[group, :], b[group, :]
                a0, a1 = ga[s:s + 1], ga[s + 1:s + 2]
                b0, b1 = gb[s:s + 1], gb[s + 1:s + 2]
                p, q = a0[:, s:s + 1], a0[:, s + 1:s + 2]
                q2, r = a1[:, s:s + 1], a1[:, s + 1:s + 2]
                inv = 1.0 / (p * r - q * q2)
                p, q, q2, r = p * inv, q * inv, q2 * inv, r * inv
                na0, na1 = r * a0 - q * a1, p * a1 - q2 * a0
                nb0, nb1 = r * b0 - q * b1, p * b1 - q2 * b0
                old = a[...]
                c0, c1 = old[:, s:s + 1], old[:, s + 1:s + 2]
                a[...] = old - c0 * na0 - c1 * na1
                b[...] = b[...] - c0 * nb0 - c1 * nb1
                a[group, :] = jnp.where(sub == s, na0, jnp.where(sub == s + 1, na1, a[group, :]))
                b[group, :] = jnp.where(sub == s, nb0, jnp.where(sub == s + 1, nb1, b[group, :]))
            a[...] = pltpu.roll(a[...], fr - 8, 1)
            return c

        lax.fori_loop(0, fr // 8, block, 0)
        x = b[...]
        prop[...] = x[0:fr - 1, 1:fr]
        adv = jnp.where(col == 0, jnp.where(row == 0, 1.0, 0.0), x)
        mh, ml = split(adv)
        m[0:fr, 0:fr] = mh
        m[0:fr, fr:2 * fr] = ml
        m[fr:2 * fr, 0:fr] = mh
        m[fr:2 * fr, fr:2 * fr] = jnp.zeros((fr, fr), BF16)

    for y in range(filt.shape[1]):
        v = jnp.dot(filt[0, y], m[...], preferred_element_type=F32)
        out[0, y] = (v[:, 0:fr] + v[:, fr:2 * fr]).astype(BF16)


def on_device(nx, ny, movie, brain_mask):
    cx, cy, cz, fr = movie.shape
    r = fr // ny
    vmem = pl.BlockSpec(memory_space=pltpu.VMEM)
    dma = pltpu.SemaphoreType.DMA
    filt, gram = pl.pallas_call(
        functools.partial(filter_kernel, nx, ny),
        out_shape=(
            jax.ShapeDtypeStruct((cx, cy, cz, 2 * fr), BF16),
            jax.ShapeDtypeStruct((ny, r, fr), F32),
        ),
        in_specs=[vmem, vmem],
        out_specs=(vmem, vmem),
        scratch_shapes=[
            pltpu.VMEM((cx, RAD, cz, fr), BF16),
            pltpu.VMEM((cx, RAD, cz, fr), BF16),
            pltpu.VMEM((cx, cy, cz, fr), BF16),
            pltpu.VMEM((RAD, cy, cz, fr), BF16),
            pltpu.VMEM((RAD, cy, cz, fr), BF16),
            pltpu.VMEM((cx + 2 * RAD, cy, cz, fr), F32),
            pltpu.VMEM((cy, cz, fr), F32),
            pltpu.VMEM((cz, 3 * cz), BF16),
            pltpu.VMEM((cz, cx * cy), BF16),
            pltpu.VMEM((fr, 2 * fr), F32),
            pltpu.VMEM((ny, r, fr), F32),
            pltpu.VMEM((ny, r, fr), F32),
            pltpu.VMEM((nx, r, fr), F32),
            pltpu.VMEM((ny, r, fr), F32),
            dma((cx,)), dma((cx,)), dma((cx,)), dma((cx,)),
            dma((RAD,)), dma((RAD,)), dma((RAD,)), dma((RAD,)),
            dma((ny,)), dma((ny,)), dma((nx,)), dma((nx,)), dma((ny,)), dma((ny,)),
        ],
        compiler_params=pltpu.CompilerParams(
            collective_id=0, has_side_effects=True, vmem_limit_bytes=48 * 1024 * 1024),
    )(movie, brain_mask)
    gram = gram.reshape(fr, fr)
    fitted, propagator = pl.pallas_call(
        fit_kernel,
        grid=(cx,),
        out_shape=(
            jax.ShapeDtypeStruct((cx, cy, cz, fr), BF16),
            jax.ShapeDtypeStruct((fr - 1, fr - 1), F32),
        ),
        in_specs=[
            pl.BlockSpec((fr, fr), lambda i: (0, 0)),
            pl.BlockSpec((1, cy, cz, 2 * fr), lambda i: (i, 0, 0, 0)),
        ],
        out_specs=(
            pl.BlockSpec((1, cy, cz, fr), lambda i: (i, 0, 0, 0)),
            pl.BlockSpec((fr - 1, fr - 1), lambda i: (0, 0)),
        ),
        scratch_shapes=[
            pltpu.VMEM((fr, fr), F32),
            pltpu.VMEM((fr, fr), F32),
            pltpu.VMEM((2 * fr, 2 * fr), BF16),
        ],
        compiler_params=pltpu.CompilerParams(vmem_limit_bytes=32 * 1024 * 1024),
    )(gram, filt)
    return fitted, propagator


def solution(mesh):
    nx, ny = mesh.shape["gx"], mesh.shape["gy"]
    return jax.shard_map(
        functools.partial(on_device, nx, ny),
        mesh=mesh,
        in_specs=(P("gx", "gy", None, None), P("gx", "gy", None)),
        out_specs=(P("gx", "gy", None, None), P()),
        check_vma=False,
    )
```

time: 390 us -> 84.7 us (0.22)
  waiting for transfers between devices: 184 us -> 0 us
  other arithmetic: 152 us -> 0 us
  Pallas kernels: 0 us -> 79.2 us
  matrix products: 17.6 us -> 0 us
  between operations: 14.9 us -> 0.66 us
  starting transfers between devices: 9.04 us -> 0 us
  local copies, waits for them, and re-layouts: 10.2 us -> 4.52 us
    psum x1 -> x0, waiting for transfers between devices: 157 us -> none  [on_device(): gram = lax.psum(local_gram, ('gx', 'gy'))]
    add x3 -> x0, other arithmetic: 108 us -> none  [the longest x2 107 us: taps_along(): total + weights[k] * lax.slice_in_dim(field, k, k + length, axis=axis)]
    pallas_call x0 -> x2, Pallas kernels: none -> 79.2 us  [the longest x1 53.7 us: on_device(): pl.pallas_call(functools.partial(filter_kernel, nx, ny), out_shape=(jax.S...]
    ppermute x4 -> x0, waiting for transfers between devices: 27.5 us -> none  [the longest x2 21.4 us: extended(): before = lax.ppermute(last, axis, up)]
    another operation x6 -> x0, other arithmetic: 23.4 us -> none  [the longest x3 12.3 us: on_device(): jnp.linalg.cholesky(g_left + lam * jnp.eye(frames - 1, dtype=jnp.float32))]
    dot_general x2 -> x0, matrix products: 13.7 us -> none  [the longest x1 7.56 us: on_device(): lax.dot_general(filtered, filtered, (((0,), (0,)), ((), ())), precision=l...]
    mul x1 -> x0, other arithmetic: 10.5 us -> none  [on_device(): filtered = (mask_f * (movie.astype(jnp.float32) - blur)).reshape(-1, frames)]
    ppermute x4 -> x0, starting transfers between devices: 9 us -> none  [the longest x2 6.42 us: extended(): before = lax.ppermute(last, axis, up)]
  transfers between devices with their start and end apart: 5 -> 0, of which waited for: 5 -> 0; matrix products, arithmetic and copies ran while one was open for 1% -> 0% of each run, Pallas kernels for 0% -> 0%
where the time goes in v1:
time: 84.7 us; the launch traced here: 84.4 us
  Pallas kernels  79.2 us (94%)
  local copies, waits for them, and re-layouts  4.52 us (5%)
    pallas_call x1, Pallas kernels, on_device(): pl.pallas_call(functools.partial(filter_kernel, nx, ny), out_shape=(jax.S...  53.7 us
    pallas_call x1, Pallas kernels, on_device(): pl.pallas_call(fit_kernel, grid=(cx,), out_shape=(jax.ShapeDtypeStruct((c...  25.6 us
    unnamed x6, local copies, waits for them, and re-layouts  4.52 us

profile of v1, /device:TPU:0, one launch (start us, length us, event | category | flops | bytes accessed | tf_op | source)
XLA Modules:
  0.0 84.4 jit_solution(16080454658073858342)
XLA Ops:
  0.6 0.0 copy-start.1
  0.6 1.6 %copy-done.1 = bf16[8,8,128,128]{3,2,1,0:T(8,128)(2,1)S(1)} copy-done((bf16[8,8,128,128]{3,2,1,0:T(8,128)(2,1)S(1)}, bf16[8,8,128,128]{3,2,1,0:T(8,128)(2,1)}, u32[]{:S(2)}) %copy-start.1) | copy-done | bytes 2097176
  2.2 0.0 copy-start.2
  2.2 0.8 copy-done.2
  3.0 53.7 %shard_map.41 = (bf16[8,8,128,256]{3,2,1,0:T(8,128)(2,1)}, f32[8,16,128]{2,1,0:T(8,128)S(1)}) custom-call(bf16[8,8,128,128]{3,2,1,0:T(8,128)(2,1)S(1)} %copy-done.1, s32[8,8,128]{2,1,0:T(8,128)S(1)} %copy-done.2), custom_call_target="tpu_custom_call" | custom-call | tf_op jit(solution)/shard_map/pallas_call | solution.py:352
  56.7 0.0 copy-start
  56.7 2.2 %copy-done = bf16[8,8,128,256]{3,2,1,0:T(8,128)(2,1)S(1)} copy-done((bf16[8,8,128,256]{3,2,1,0:T(8,128)(2,1)S(1)}, bf16[8,8,128,256]{3,2,1,0:T(8,128)(2,1)}, u32[]{:S(2)}) %copy-start) | copy-done | bytes 4194328
  58.9 25.6 %shard_map.42 = (bf16[8,8,128,128]{3,2,1,0:T(8,128)(2,1)}, f32[127,127]{1,0:T(8,128)}) custom-call(f32[128,128]{1,0:T(8,128)S(1)} %bitcast.1, bf16[8,8,128,256]{3,2,1,0:T(8,128)(2,1)S(1)} %copy-done), custom_call_target="tpu_custom_call" | custom-call | tf_op jit(solution)/shard_map/pallas_call | solution.py:383
Async XLA Ops:
  0.6 1.6 %copy-start.1 = (bf16[8,8,128,128]{3,2,1,0:T(8,128)(2,1)S(1)}, bf16[8,8,128,128]{3,2,1,0:T(8,128)(2,1)}, u32[]{:S(2)}) copy-start(bf16[8,8,128,128]{3,2,1,0:T(8,128)(2,1)} %movie.1) | copy-start | bytes 6291460
  2.2 0.8 copy-start.2
  56.7 2.2 %copy-start = (bf16[8,8,128,256]{3,2,1,0:T(8,128)(2,1)S(1)}, bf16[8,8,128,256]{3,2,1,0:T(8,128)(2,1)}, u32[]{:S(2)}) copy-start(bf16[8,8,128,256]{3,2,1,0:T(8,128)(2,1)} %get-tuple-element.5.filt) | copy-start | bytes 12582916

commit v2 on v1

--- a/solution.py
+++ b/solution.py
@@ -39,12 +39,16 @@
 
 def filter_kernel(
     nx, ny,
-    movie, mask, filt, gram_out,
-    ylo, yhi, ysend, xlo, xhi, yb, xb, band, maskt, gacc, gpart, rsbuf, xbuf, gfull,
+    movie_hbm, mask_hbm, filt, gram_out,
+    movie, mask, local, ylo, yhi, ysend, xlo, xhi, yb, xb, band, maskt, gacc, gpart, rsbuf, xbuf, gfull,
     ysl, ysh, yrl, yrh, xsl, xsh, xrl, xrh, s1, r1, s2, r2, s3, r3,
 ):
     cx, cy, cz, fr = movie.shape
     gx, gy = lax.axis_index("gx"), lax.axis_index("gy")
+    load_movie = pltpu.make_async_copy(movie_hbm, movie, local.at[0])
+    load_mask = pltpu.make_async_copy(mask_hbm, mask, local.at[1])
+    load_movie.start()
+    load_mask.start()
     barrier = pltpu.get_barrier_semaphore()
 
     def hello_y(d, c):
@@ -67,13 +71,13 @@
 
     def y_up(l):
         return pltpu.make_async_remote_copy(
-            src_ref=movie.at[l, pl.ds(cy - RAD, RAD)], dst_ref=ylo.at[l],
+            src_ref=movie_hbm.at[l, pl.ds(cy - RAD, RAD)], dst_ref=ylo.at[l],
             send_sem=ysl.at[l], recv_sem=yrl.at[l],
             device_id=(gx, gy + 1), device_id_type=MESH)
 
     def y_down(l):
         return pltpu.make_async_remote_copy(
-            src_ref=movie.at[l, pl.ds(0, RAD)], dst_ref=yhi.at[l],
+            src_ref=movie_hbm.at[l, pl.ds(0, RAD)], dst_ref=yhi.at[l],
             send_sem=ysh.at[l], recv_sem=yrh.at[l],
             device_id=(gx, gy - 1), device_id_type=MESH)
 
@@ -127,9 +131,11 @@
     band[:, 0:cz] = th
     band[:, cz:2 * cz] = tl
     band[:, 2 * cz:3 * cz] = th
+    load_mask.wait()
     maskt[...] = jnp.transpose(mask[...].astype(F32).reshape(cx * cy, cz)).astype(BF16)
     gacc[...] = jnp.zeros_like(gacc)
 
+    load_movie.wait()
     ZT = 16
 
     def y_layer(i, c):
@@ -293,7 +299,52 @@
     lax.fori_loop(0, RAD, drain_x, 0)
 
 
-def fit_kernel(gram, filt, out, prop, a, b, m):
+BLK = 8
+
+
+def sweep_block(a, dbuf, zbuf, start):
+    n = a.shape[0]
+    row = lax.broadcasted_iota(jnp.int32, (n, n), 1)
+    lane = lax.broadcasted_iota(jnp.int32, (BLK, n), 1)
+    sub = lax.broadcasted_iota(jnp.int32, (BLK, n), 0)
+    inside = (lane >= start) & (lane < start + BLK)
+    panel = a[start:start + BLK, :]
+    u = jnp.where(inside, 0.0, panel)
+    zbuf[...] = jnp.where(lane == start + sub, -1.0, u)
+    for j in range(BLK):
+        dbuf[j] = jnp.broadcast_to(panel[:, start + j:start + j + 1], (BLK, n))
+    d = {(i, j): jnp.broadcast_to(dbuf[j, i:i + 1, :], (BLK, n)) for j in range(BLK) for i in range(j + 1)}
+    z = [jnp.broadcast_to(zbuf[i:i + 1, :], (BLK, n)) for i in range(BLK)]
+    inverses, multipliers = {}, {}
+    for s in range(0, BLK, 2):
+        p, q, r = d[s, s], d[s, s + 1], d[s + 1, s + 1]
+        inv = 1.0 / (p * r - q * q)
+        ip, iq, ir = r * inv, -(q * inv), p * inv
+        inverses[s] = (ip, iq, ir)
+        for i in range(s + 2, BLK):
+            m0 = d[s, i] * ip + d[s + 1, i] * iq
+            m1 = d[s, i] * iq + d[s + 1, i] * ir
+            multipliers[s, i] = (m0, m1)
+            for j in range(i, BLK):
+                d[i, j] = d[i, j] - (m0 * d[s, j] + m1 * d[s + 1, j])
+            z[i] = z[i] - (m0 * z[s] + m1 * z[s + 1])
+    for s in range(BLK - 2, -1, -2):
+        ip, iq, ir = inverses[s]
+        w0, w1 = ip * z[s] + iq * z[s + 1], iq * z[s] + ir * z[s + 1]
+        for i in range(BLK - 1, s + 1, -1):
+            m0, m1 = multipliers[s, i]
+            w0, w1 = w0 - m0 * z[i], w1 - m1 * z[i]
+        z[s], z[s + 1] = w0, w1
+    full = z[0]
+    for i in range(1, BLK):
+        full = jnp.where(sub == i, z[i], full)
+    update = lax.dot_general(
+        u, full, (((0,), (0,)), ((), ())), precision=lax.Precision.HIGHEST, preferred_element_type=F32)
+    a[...] = jnp.where((row >= start) & (row < start + BLK), 0.0, a[...]) - update
+    a[start:start + BLK, :] = full
+
+
+def fit_kernel(gram, filt, out, prop, a, m, dbuf, zbuf):
     fr = gram.shape[0]
 
     @pl.when(pl.program_id(0) == 0)
@@ -303,34 +354,13 @@
         col = lax.broadcasted_iota(jnp.int32, (fr, fr), 1)
         diag = jnp.where((row == col) & (row < fr - 1), g, 0.0)
         lam = 0.5 * jnp.sum(diag) / (fr - 1)
+        scaled = g / lam
         last = (row == fr - 1) | (col == fr - 1)
-        a[...] = jnp.where(last, 0.0, g) + jnp.where(row == col, lam, 0.0)
-        b[...] = jnp.where(row == fr - 1, 0.0, g)
-
-        def block(i, c):
-            group = pl.ds(pl.multiple_of(i * 8, 8), 8)
-            sub = lax.broadcasted_iota(jnp.int32, (8, fr), 0)
-            for s in range(0, 8, 2):
-                ga, gb = a[group, :], b[group, :]
-                a0, a1 = ga[s:s + 1], ga[s + 1:s + 2]
-                b0, b1 = gb[s:s + 1], gb[s + 1:s + 2]
-                p, q = a0[:, s:s + 1], a0[:, s + 1:s + 2]
-                q2, r = a1[:, s:s + 1], a1[:, s + 1:s + 2]
-                inv = 1.0 / (p * r - q * q2)
-                p, q, q2, r = p * inv, q * inv, q2 * inv, r * inv
-                na0, na1 = r * a0 - q * a1, p * a1 - q2 * a0
-                nb0, nb1 = r * b0 - q * b1, p * b1 - q2 * b0
-                old = a[...]
-                c0, c1 = old[:, s:s + 1], old[:, s + 1:s + 2]
-                a[...] = old - c0 * na0 - c1 * na1
-                b[...] = b[...] - c0 * nb0 - c1 * nb1
-                a[group, :] = jnp.where(sub == s, na0, jnp.where(sub == s + 1, na1, a[group, :]))
-                b[group, :] = jnp.where(sub == s, nb0, jnp.where(sub == s + 1, nb1, b[group, :]))
-            a[...] = pltpu.roll(a[...], fr - 8, 1)
-            return c
-
-        lax.fori_loop(0, fr // 8, block, 0)
-        x = b[...]
+        a[...] = jnp.where(last, 0.0, scaled) + jnp.where(row == col, 1.0, 0.0)
+        for start in range(0, fr, BLK):
+            sweep_block(a, dbuf, zbuf, start)
+        x = -jnp.dot(a[...], jnp.where(row == fr - 1, 0.0, scaled),
+                     precision=lax.Precision.HIGHEST, preferred_element_type=F32)
         prop[...] = x[0:fr - 1, 1:fr]
         adv = jnp.where(col == 0, jnp.where(row == 0, 1.0, 0.0), x)
         mh, ml = split(adv)
@@ -339,8 +369,9 @@
         m[fr:2 * fr, 0:fr] = mh
         m[fr:2 * fr, fr:2 * fr] = jnp.zeros((fr, fr), BF16)
 
+    i = pl.program_id(0)
     for y in range(filt.shape[1]):
-        v = jnp.dot(filt[0, y], m[...], preferred_element_type=F32)
+        v = jnp.dot(filt[i, y], m[...], preferred_element_type=F32)
         out[0, y] = (v[:, 0:fr] + v[:, fr:2 * fr]).astype(BF16)
 
 
@@ -348,6 +379,7 @@
     cx, cy, cz, fr = movie.shape
     r = fr // ny
     vmem = pl.BlockSpec(memory_space=pltpu.VMEM)
+    hbm = pl.BlockSpec(memory_space=pltpu.HBM)
     dma = pltpu.SemaphoreType.DMA
     filt, gram = pl.pallas_call(
         functools.partial(filter_kernel, nx, ny),
@@ -355,9 +387,12 @@
             jax.ShapeDtypeStruct((cx, cy, cz, 2 * fr), BF16),
             jax.ShapeDtypeStruct((ny, r, fr), F32),
         ),
-        in_specs=[vmem, vmem],
+        in_specs=[hbm, hbm],
         out_specs=(vmem, vmem),
         scratch_shapes=[
+            pltpu.VMEM((cx, cy, cz, fr), BF16),
+            pltpu.VMEM((cx, cy, cz), jnp.int32),
+            dma((2,)),
             pltpu.VMEM((cx, RAD, cz, fr), BF16),
             pltpu.VMEM((cx, RAD, cz, fr), BF16),
             pltpu.VMEM((cx, cy, cz, fr), BF16),
@@ -377,7 +412,7 @@
             dma((ny,)), dma((ny,)), dma((nx,)), dma((nx,)), dma((ny,)), dma((ny,)),
         ],
         compiler_params=pltpu.CompilerParams(
-            collective_id=0, has_side_effects=True, vmem_limit_bytes=48 * 1024 * 1024),
+            collective_id=0, has_side_effects=True, vmem_limit_bytes=28 * 1024 * 1024),
     )(movie, brain_mask)
     gram = gram.reshape(fr, fr)
     fitted, propagator = pl.pallas_call(
@@ -389,7 +424,7 @@
         ),
         in_specs=[
             pl.BlockSpec((fr, fr), lambda i: (0, 0)),
-            pl.BlockSpec((1, cy, cz, 2 * fr), lambda i: (i, 0, 0, 0)),
+            vmem,
         ],
         out_specs=(
             pl.BlockSpec((1, cy, cz, fr), lambda i: (i, 0, 0, 0)),
@@ -397,10 +432,11 @@
         ),
         scratch_shapes=[
             pltpu.VMEM((fr, fr), F32),
-            pltpu.VMEM((fr, fr), F32),
             pltpu.VMEM((2 * fr, 2 * fr), BF16),
+            pltpu.VMEM((BLK, BLK, fr), F32),
+            pltpu.VMEM((BLK, fr), F32),
         ],
-        compiler_params=pltpu.CompilerParams(vmem_limit_bytes=32 * 1024 * 1024),
+        compiler_params=pltpu.CompilerParams(vmem_limit_bytes=16 * 1024 * 1024),
     )(gram, filt)
     return fitted, propagator
 

time: 84.7 us -> 65.9 us (0.78)
  Pallas kernels: 79.2 us -> 62.7 us
  local copies, waits for them, and re-layouts: 4.52 us -> 2.34 us
    pallas_call x1, Pallas kernels: 25.6 us -> 10.7 us  [on_device(): pl.pallas_call(fit_kernel, grid=(cx,), out_shape=(jax.ShapeDtypeStruct((c...]
    unnamed x6 -> x4, local copies, waits for them, and re-layouts: 4.52 us -> 2.34 us
    pallas_call x1, Pallas kernels: 53.7 us -> 52 us  [on_device(): pl.pallas_call(functools.partial(filter_kernel, nx, ny), out_shape=(jax.S...]
where the time goes in v2:
time: 65.9 us; the launch traced here: 65.7 us
  Pallas kernels  62.7 us (95%)
  local copies, waits for them, and re-layouts  2.34 us (4%)
    pallas_call x1, Pallas kernels, on_device(): pl.pallas_call(functools.partial(filter_kernel, nx, ny), out_shape=(jax.S...  52 us
    pallas_call x1, Pallas kernels, on_device(): pl.pallas_call(fit_kernel, grid=(cx,), out_shape=(jax.ShapeDtypeStruct((c...  10.7 us
    unnamed x4, local copies, waits for them, and re-layouts  2.34 us

profile of v2, /device:TPU:0, one launch (start us, length us, event | category | flops | bytes accessed | tf_op | source)
XLA Modules:
  0.0 65.7 jit_solution(2381021917526690402)
XLA Ops:
  0.6 0.0 copy-start
  0.6 1.6 %copy-done = bf16[8,8,128,128]{3,2,1,0:T(8,128)(2,1)S(1)} copy-done((bf16[8,8,128,128]{3,2,1,0:T(8,128)(2,1)S(1)}, bf16[8,8,128,128]{3,2,1,0:T(8,128)(2,1)}, u32[]{:S(2)}) %copy-start) | copy-done | bytes 2097176
  2.2 0.0 copy-start.1
  2.2 0.8 %copy-done.1 = s32[8,8,128]{2,1,0:T(8,128)S(1)} copy-done((s32[8,8,128]{2,1,0:T(8,128)S(1)}, s32[8,8,128]{2,1,0:T(8,128)}, u32[]{:S(2)}) %copy-start.1) | copy-done | bytes 32792
  3.0 52.0 %shard_map.41 = (bf16[8,8,128,256]{3,2,1,0:T(8,128)(2,1)S(1)}, f32[8,16,128]{2,1,0:T(8,128)S(1)}) custom-call(bf16[8,8,128,128]{3,2,1,0:T(8,128)(2,1)S(1)} %copy-done, s32[8,8,128]{2,1,0:T(8,128)S(1)} %copy-done.1), custom_call_target="tpu_custom_call" | custom-call | tf_op jit(solution)/shard_map/pallas_call | solution.py:384
  55.0 10.7 %shard_map.42 = (bf16[8,8,128,128]{3,2,1,0:T(8,128)(2,1)}, f32[127,127]{1,0:T(8,128)}) custom-call(f32[128,128]{1,0:T(8,128)S(1)} %bitcast.1, bf16[8,8,128,256]{3,2,1,0:T(8,128)(2,1)S(1)} %get-tuple-element.5.filt), custom_call_target="tpu_custom_call" | custom-call | tf_op jit(solution)/shard_map/pallas_call | solution.py:418
Async XLA Ops:
  0.6 1.6 %copy-start = (bf16[8,8,128,128]{3,2,1,0:T(8,128)(2,1)S(1)}, bf16[8,8,128,128]{3,2,1,0:T(8,128)(2,1)}, u32[]{:S(2)}) copy-start(bf16[8,8,128,128]{3,2,1,0:T(8,128)(2,1)} %movie_hbm.1) | copy-start | bytes 6291460
  2.2 0.8 %copy-start.1 = (s32[8,8,128]{2,1,0:T(8,128)S(1)}, s32[8,8,128]{2,1,0:T(8,128)}, u32[]{:S(2)}) copy-start(s32[8,8,128]{2,1,0:T(8,128)} %mask_hbm.1) | copy-start | bytes 98308

commit v3 on v2

--- a/solution.py
+++ b/solution.py
@@ -39,8 +39,8 @@
 
 def filter_kernel(
     nx, ny,
-    movie_hbm, mask_hbm, filt, gram_out,
-    movie, mask, local, ylo, yhi, ysend, xlo, xhi, yb, xb, band, maskt, gacc, gpart, rsbuf, xbuf, gfull,
+    movie_hbm, mask_hbm, filt_hbm, gram_out,
+    movie, mask, local, filt, fsem, ylo, yhi, ysend, xlo, xhi, zy, yb, maskx, band, maskt, gacc, gpart, rsbuf, xbuf, gfull,
     ysl, ysh, yrl, yrh, xsl, xsh, xrl, xrh, s1, r1, s2, r2, s3, r3,
 ):
     cx, cy, cz, fr = movie.shape
@@ -138,6 +138,27 @@
     load_movie.wait()
     ZT = 16
 
+    def z_pair(pieces, lhs, to, y):
+        v = jnp.dot(lhs, jnp.concatenate(pieces, axis=0), preferred_element_type=F32)
+        zy[to, y] = v[:, 0:fr]
+        zy[to, y + 1] = v[:, fr:2 * fr]
+
+    def halo_layer(src, j, to):
+        for y in range(0, cy, 2):
+            h = jnp.concatenate([src[j, y], src[j, y + 1]], axis=1)
+            z_pair([h, h], band[:, 0:2 * cz], to, y)
+
+    def halo_step(j):
+        @pl.when(has_xl)
+        def _():
+            x_up(RAD - 1 - j).wait_recv()
+
+        @pl.when(has_xh)
+        def _():
+            x_down(j).wait_recv()
+        halo_layer(xlo, RAD - 1 - j, RAD - 1 - j)
+        halo_layer(xhi, j, cx + RAD + j)
+
     def y_layer(i, c):
         l = order(i)
 
@@ -156,7 +177,7 @@
             items += [yhi[l, k, rows, :].astype(F32) for k in range(RAD)]
             for y in range(cy):
                 v = blur9(items, y)
-                yb[l + RAD, y, rows, :] = v
+                yb[y, rows, :] = v
                 ysend[l, y, rows, :] = v.astype(BF16)
             return c2
 
@@ -169,56 +190,42 @@
         @pl.when(jnp.logical_and(i % 2 == 1, has_xh))
         def _():
             x_up(RAD - 1 - i // 2).start()
+
+        lanes = lax.broadcasted_iota(jnp.int32, (cx * cy, fr), 0)
+        for y in range(0, cy, 2):
+            parts = [split(yb[y + k]) for k in range(2)]
+            hi = jnp.concatenate([p[0] for p in parts], axis=1)
+            lo = jnp.concatenate([p[1] for p in parts], axis=1)
+            z_pair([hi, hi, lo], band[...], l + RAD, y)
+            for k in range(2):
+                one = jnp.where(lanes == l * cy + y + k, 1.0, 0.0).astype(BF16)
+                maskx[l, y + k] = jnp.dot(maskt[...], one, preferred_element_type=F32).astype(BF16)
+
         return c
 
     lax.fori_loop(0, cx, y_layer, 0)
 
-    def widen(src, j, to):
-        def tile(z, c):
-            rows = pl.ds(pl.multiple_of(z * ZT, ZT), ZT)
-            for y in range(cy):
-                yb[to, y, rows, :] = src[j, y, rows, :].astype(F32)
-            return c
-        lax.fori_loop(0, cz // ZT, tile, 0)
+    def save(l):
+        return pltpu.make_async_copy(filt.at[l], filt_hbm.at[l], fsem.at[l])
 
     def x_layer(l):
         def tile(z, c):
             rows = pl.ds(pl.multiple_of(z * ZT, ZT), ZT)
             for y in range(cy):
-                items = [yb[l + k, y, rows, :] for k in range(2 * RAD + 1)]
-                xb[y, rows, :] = blur9(items, 0)
+                blur = blur9([zy[l + k, y, rows, :] for k in range(2 * RAD + 1)], 0)
+                f = maskx[l, y, rows, :].astype(F32) * (movie[l, y, rows, :].astype(F32) - blur)
+                fh, fl = split(f)
+                filt[l, y, rows, 0:fr] = fh
+                filt[l, y, rows, fr:2 * fr] = fl
             return c
         lax.fori_loop(0, cz // ZT, tile, 0)
-        lanes = lax.broadcasted_iota(jnp.int32, (cx * cy, fr), 0)
-        for y in range(0, cy, 2):
-            parts = [split(xb[y + k]) for k in range(2)]
-            hi = jnp.concatenate([p[0] for p in parts], axis=1)
-            lo = jnp.concatenate([p[1] for p in parts], axis=1)
-            blur = jnp.dot(band[...], jnp.concatenate([hi, hi, lo], axis=0), preferred_element_type=F32)
-            left, right = [], []
-            for k in range(2):
-                one = jnp.where(lanes == l * cy + y + k, 1.0, 0.0).astype(BF16)
-                m = jnp.dot(maskt[...], one, preferred_element_type=F32)
-                f = m * (movie[l, y + k].astype(F32) - blur[:, k * fr:(k + 1) * fr])
-                fh, fl = split(f)
-                both = jnp.concatenate([fh, fl], axis=1)
-                filt[l, y + k] = both
-                left.append(fh)
-                right.append(both)
-            gacc[...] += lax.dot_general(
-                jnp.concatenate(left, axis=0), jnp.concatenate(right, axis=0),
-                (((0,), (0,)), ((), ())), preferred_element_type=F32)
+        save(l).start()
+        both = filt[l].reshape(cy * cz, 2 * fr)
+        gacc[...] += lax.dot_general(
+            both[:, 0:fr], both, (((0,), (0,)), ((), ())), preferred_element_type=F32)
 
     def x_step(j, c):
-        @pl.when(has_xl)
-        def _():
-            x_up(RAD - 1 - j).wait_recv()
-
-        @pl.when(has_xh)
-        def _():
-            x_down(j).wait_recv()
-        widen(xlo, RAD - 1 - j, RAD - 1 - j)
-        widen(xhi, j, cx + RAD + j)
+        halo_step(j)
 
         def two(s, c2):
             x_layer(jnp.where(s == 0, RAD - 1 - j, cx - RAD + j))
@@ -295,6 +302,11 @@
             x_down(j).wait_send()
         return c
 
+    def drain_f(l, c):
+        save(l).wait()
+        return c
+
+    lax.fori_loop(0, cx, drain_f, 0)
     lax.fori_loop(0, cx, drain_y, 0)
     lax.fori_loop(0, RAD, drain_x, 0)
 
@@ -344,35 +356,49 @@
     a[start:start + BLK, :] = full
 
 
-def fit_kernel(gram, filt, out, prop, a, m, dbuf, zbuf):
+def fit_kernel(gram, filt_hbm, out_hbm, prop, a, m, dbuf, zbuf, filt, out, isem, osem):
     fr = gram.shape[0]
-
-    @pl.when(pl.program_id(0) == 0)
-    def _():
-        g = gram[...]
-        row = lax.broadcasted_iota(jnp.int32, (fr, fr), 0)
-        col = lax.broadcasted_iota(jnp.int32, (fr, fr), 1)
-        diag = jnp.where((row == col) & (row < fr - 1), g, 0.0)
-        lam = 0.5 * jnp.sum(diag) / (fr - 1)
-        scaled = g / lam
-        last = (row == fr - 1) | (col == fr - 1)
-        a[...] = jnp.where(last, 0.0, scaled) + jnp.where(row == col, 1.0, 0.0)
-        for start in range(0, fr, BLK):
-            sweep_block(a, dbuf, zbuf, start)
-        x = -jnp.dot(a[...], jnp.where(row == fr - 1, 0.0, scaled),
-                     precision=lax.Precision.HIGHEST, preferred_element_type=F32)
-        prop[...] = x[0:fr - 1, 1:fr]
-        adv = jnp.where(col == 0, jnp.where(row == 0, 1.0, 0.0), x)
-        mh, ml = split(adv)
-        m[0:fr, 0:fr] = mh
-        m[0:fr, fr:2 * fr] = ml
-        m[fr:2 * fr, 0:fr] = mh
-        m[fr:2 * fr, fr:2 * fr] = jnp.zeros((fr, fr), BF16)
-
-    i = pl.program_id(0)
-    for y in range(filt.shape[1]):
-        v = jnp.dot(filt[i, y], m[...], preferred_element_type=F32)
-        out[0, y] = (v[:, 0:fr] + v[:, fr:2 * fr]).astype(BF16)
+    load = pltpu.make_async_copy(filt_hbm, filt, isem.at[0])
+    load.start()
+
+    g = gram[...]
+    row = lax.broadcasted_iota(jnp.int32, (fr, fr), 0)
+    col = lax.broadcasted_iota(jnp.int32, (fr, fr), 1)
+    diag = jnp.where((row == col) & (row < fr - 1), g, 0.0)
+    lam = 0.5 * jnp.sum(diag) / (fr - 1)
+    scaled = g / lam
+    last = (row == fr - 1) | (col == fr - 1)
+    a[...] = jnp.where(last, 0.0, scaled) + jnp.where(row == col, 1.0, 0.0)
+    for start in range(0, fr, BLK):
+        sweep_block(a, dbuf, zbuf, start)
+    x = -jnp.dot(a[...], jnp.where(row == fr - 1, 0.0, scaled),
+                 precision=lax.Precision.HIGHEST, preferred_element_type=F32)
+    prop[...] = x[0:fr - 1, 1:fr]
+    adv = jnp.where(col == 0, jnp.where(row == 0, 1.0, 0.0), x)
+    mh, ml = split(adv)
+    m[0:fr, 0:fr] = mh
+    m[0:fr, fr:2 * fr] = ml
+    m[fr:2 * fr, 0:fr] = mh
+    m[fr:2 * fr, fr:2 * fr] = jnp.zeros((fr, fr), BF16)
+
+    load.wait()
+
+    def save(i):
+        return pltpu.make_async_copy(out.at[i], out_hbm.at[i], osem.at[i])
+
+    def layer(i, c):
+        for y in range(filt.shape[1]):
+            v = jnp.dot(filt[i, y], m[...], preferred_element_type=F32)
+            out[i, y] = (v[:, 0:fr] + v[:, fr:2 * fr]).astype(BF16)
+        save(i).start()
+        return c
+
+    def drain(i, c):
+        save(i).wait()
+        return c
+
+    lax.fori_loop(0, filt.shape[0], layer, 0)
+    lax.fori_loop(0, filt.shape[0], drain, 0)
 
 
 def on_device(nx, ny, movie, brain_mask):
@@ -388,11 +414,13 @@
             jax.ShapeDtypeStruct((ny, r, fr), F32),
         ),
         in_specs=[hbm, hbm],
-        out_specs=(vmem, vmem),
+        out_specs=(hbm, vmem),
         scratch_shapes=[
             pltpu.VMEM((cx, cy, cz, fr), BF16),
             pltpu.VMEM((cx, cy, cz), jnp.int32),
             dma((2,)),
+            pltpu.VMEM((cx, cy, cz, 2 * fr), BF16),
+            dma((cx,)),
             pltpu.VMEM((cx, RAD, cz, fr), BF16),
             pltpu.VMEM((cx, RAD, cz, fr), BF16),
             pltpu.VMEM((cx, cy, cz, fr), BF16),
@@ -400,6 +428,7 @@
             pltpu.VMEM((RAD, cy, cz, fr), BF16),
             pltpu.VMEM((cx + 2 * RAD, cy, cz, fr), F32),
             pltpu.VMEM((cy, cz, fr), F32),
+            pltpu.VMEM((cx, cy, cz, fr), BF16),
             pltpu.VMEM((cz, 3 * cz), BF16),
             pltpu.VMEM((cz, cx * cy), BF16),
             pltpu.VMEM((fr, 2 * fr), F32),
@@ -412,31 +441,28 @@
             dma((ny,)), dma((ny,)), dma((nx,)), dma((nx,)), dma((ny,)), dma((ny,)),
         ],
         compiler_params=pltpu.CompilerParams(
-            collective_id=0, has_side_effects=True, vmem_limit_bytes=28 * 1024 * 1024),
+            collective_id=0, has_side_effects=True, vmem_limit_bytes=60 * 1024 * 1024),
     )(movie, brain_mask)
     gram = gram.reshape(fr, fr)
     fitted, propagator = pl.pallas_call(
         fit_kernel,
-        grid=(cx,),
         out_shape=(
             jax.ShapeDtypeStruct((cx, cy, cz, fr), BF16),
             jax.ShapeDtypeStruct((fr - 1, fr - 1), F32),
         ),
-        in_specs=[
-            pl.BlockSpec((fr, fr), lambda i: (0, 0)),
-            vmem,
-        ],
-        out_specs=(
-            pl.BlockSpec((1, cy, cz, fr), lambda i: (i, 0, 0, 0)),
-            pl.BlockSpec((fr - 1, fr - 1), lambda i: (0, 0)),
-        ),
+        in_specs=[vmem, hbm],
+        out_specs=(hbm, vmem),
         scratch_shapes=[
             pltpu.VMEM((fr, fr), F32),
             pltpu.VMEM((2 * fr, 2 * fr), BF16),
             pltpu.VMEM((BLK, BLK, fr), F32),
             pltpu.VMEM((BLK, fr), F32),
+            pltpu.VMEM((cx, cy, cz, 2 * fr), BF16),
+            pltpu.VMEM((cx, cy, cz, fr), BF16),
+            dma((1,)),
+            dma((cx,)),
         ],
-        compiler_params=pltpu.CompilerParams(vmem_limit_bytes=16 * 1024 * 1024),
+        compiler_params=pltpu.CompilerParams(vmem_limit_bytes=60 * 1024 * 1024),
     )(gram, filt)
     return fitted, propagator
 

time: 65.9 us -> 61.2 us (0.929)
  local copies, waits for them, and re-layouts: 2.34 us -> 0 us
  Pallas kernels: 62.7 us -> 60.4 us
    pallas_call x1, Pallas kernels: 52 us -> 49.3 us  [on_device(): pl.pallas_call(functools.partial(filter_kernel, nx, ny), out_shape=(jax.S...]
    unnamed x4 -> x0, local copies, waits for them, and re-layouts: 2.34 us -> none
where the time goes in v3:
time: 61.2 us; the launch traced here: 61 us
  Pallas kernels  60.4 us (99%)
  between operations  0.64 us (1%)
    pallas_call x1, Pallas kernels, on_device(): pl.pallas_call(functools.partial(filter_kernel, nx, ny), out_shape=(jax.S...  49.3 us
    pallas_call x1, Pallas kernels, on_device(): pl.pallas_call(fit_kernel, out_shape=(jax.ShapeDtypeStruct((cx, cy, cz, f...  11.1 us

profile of v3, /device:TPU:0, one launch (start us, length us, event | category | flops | bytes accessed | tf_op | source)
XLA Modules:
  0.0 61.0 jit_solution(13673319019815365214)
XLA Ops:
  0.6 49.3 %shard_map.41 = (bf16[8,8,128,256]{3,2,1,0:T(8,128)(2,1)}, f32[8,16,128]{2,1,0:T(8,128)}) custom-call(bf16[8,8,128,128]{3,2,1,0:T(8,128)(2,1)} %movie_hbm.1, s32[8,8,128]{2,1,0:T(8,128)} %mask_hbm.1), custom_call_target="tpu_custom_call" | custom-call | tf_op jit(solution)/shard_map/pallas_call | solution.py:410
  49.9 11.1 %shard_map.42 = (bf16[8,8,128,128]{3,2,1,0:T(8,128)(2,1)}, f32[127,127]{1,0:T(8,128)}) custom-call(f32[128,128]{1,0:T(8,128)} %bitcast.1, bf16[8,8,128,256]{3,2,1,0:T(8,128)(2,1)} %get-tuple-element.5.filt_hbm), custom_call_target="tpu_custom_call" | custom-call | tf_op jit(solution)/shard_map/pallas_call | solution.py:447

commit v4 on v3

v4 whole, which is shorter than its diff:
```python
import functools

import numpy as np
import jax
import jax.numpy as jnp
from jax import lax
from jax.experimental import pallas as pl
from jax.experimental.pallas import tpu as pltpu
from jax.sharding import PartitionSpec as P

RAD = 4
AHEAD = 3
MESH = pl.DeviceIdType.MESH
F32 = jnp.float32
BF16 = jnp.bfloat16


def weights():
    k = np.arange(-RAD, RAD + 1).astype(np.float32)
    sigma = RAD / 2.0
    raw = np.exp(-k * k / np.float32(2.0 * sigma * sigma)).astype(np.float32)
    w = raw / raw.sum(dtype=np.float32)
    return [float(w[RAD + j]) for j in range(RAD + 1)]


W = weights()


def blur9(items, at):
    total = W[0] * items[at + RAD]
    for k in range(1, RAD + 1):
        total = total + W[k] * (items[at + RAD - k] + items[at + RAD + k])
    return total


def split(v):
    hi = v.astype(BF16)
    return hi, (v - hi.astype(F32)).astype(BF16)


def filter_kernel(
    nx, ny,
    movie_hbm, mask_hbm, filt_hbm, gram_out,
    movie, mask, local, filt, fsem, xlo, xhi, xsend, ylo, yhi, zy, yb, maskx, band, maskt, gacc, gpart, rsbuf, xbuf, gfull,
    xsl, xsh, xrl, xrh, ysl, ysh, yrl, yrh, s1, r1, s2, r2, s3, r3,
):
    cx, cy, cz, fr = movie.shape
    gx, gy = lax.axis_index("gx"), lax.axis_index("gy")
    load_movie = pltpu.make_async_copy(movie_hbm, movie, local.at[0])
    load_mask = pltpu.make_async_copy(mask_hbm, mask, local.at[1])
    load_movie.start()
    load_mask.start()
    barrier = pltpu.get_barrier_semaphore()

    def hello_y(d, c):
        pl.semaphore_signal(barrier, inc=1, device_id=(gx, lax.rem(gy + d, ny)), device_id_type=MESH)
        return c

    def hello_x(d, c):
        pl.semaphore_signal(barrier, inc=1, device_id=(lax.rem(gx + d, nx), gy), device_id_type=MESH)
        return c

    lax.fori_loop(1, ny, hello_y, 0)
    lax.fori_loop(1, nx, hello_x, 0)
    pl.semaphore_wait(barrier, ny - 1 + nx - 1)

    has_yl, has_yh = gy > 0, gy < ny - 1
    has_xl, has_xh = gx > 0, gx < nx - 1

    def order(i):
        return jnp.where(i % 2 == 0, i // 2, cy - 1 - i // 2)

    def x_up(c):
        return pltpu.make_async_remote_copy(
            src_ref=movie_hbm.at[pl.ds(cx - RAD, RAD), c], dst_ref=xlo.at[c],
            send_sem=xsl.at[c], recv_sem=xrl.at[c],
            device_id=(gx + 1, gy), device_id_type=MESH)

    def x_down(c):
        return pltpu.make_async_remote_copy(
            src_ref=movie_hbm.at[pl.ds(0, RAD), c], dst_ref=xhi.at[c],
            send_sem=xsh.at[c], recv_sem=xrh.at[c],
            device_id=(gx - 1, gy), device_id_type=MESH)

    def y_up(j):
        return pltpu.make_async_remote_copy(
            src_ref=xsend.at[cy - RAD + j], dst_ref=ylo.at[j],
            send_sem=ysl.at[j], recv_sem=yrl.at[j],
            device_id=(gx, gy + 1), device_id_type=MESH)

    def y_down(j):
        return pltpu.make_async_remote_copy(
            src_ref=xsend.at[j], dst_ref=yhi.at[j],
            send_sem=ysh.at[j], recv_sem=yrh.at[j],
            device_id=(gx, gy - 1), device_id_type=MESH)

    def start_x(i, carry):
        c = order(i)

        @pl.when(has_xh)
        def _():
            x_up(c).start()

        @pl.when(has_xl)
        def _():
            x_down(c).start()
        return carry

    lax.fori_loop(0, AHEAD, start_x, 0)

    @pl.when(jnp.logical_not(has_yl))
    def _():
        ylo[...] = jnp.zeros_like(ylo)

    @pl.when(jnp.logical_not(has_yh))
    def _():
        yhi[...] = jnp.zeros_like(yhi)

    @pl.when(jnp.logical_not(has_xl))
    def _():
        xlo[...] = jnp.zeros_like(xlo)

    @pl.when(jnp.logical_not(has_xh))
    def _():
        xhi[...] = jnp.zeros_like(xhi)

    dist = jnp.abs(lax.broadcasted_iota(jnp.int32, (cz, cz), 0) - lax.broadcasted_iota(jnp.int32, (cz, cz), 1))
    t = jnp.zeros((cz, cz), F32)
    for k in range(RAD + 1):
        t = jnp.where(dist == k, W[k], t)
    th, tl = split(t)
    band[:, 0:cz] = th
    band[:, cz:2 * cz] = tl
    band[:, 2 * cz:3 * cz] = th
    load_mask.wait()
    maskt[...] = jnp.transpose(mask[...].astype(F32).reshape(cx * cy, cz)).astype(BF16)
    gacc[...] = jnp.zeros_like(gacc)

    load_movie.wait()
    ZT = 16

    def z_pair(pieces, lhs, to, y):
        v = jnp.dot(lhs, jnp.concatenate(pieces, axis=0), preferred_element_type=F32)
        zy[to, y] = v[:, 0:fr]
        zy[to, y + 1] = v[:, fr:2 * fr]

    def halo_column(src, j, to):
        for x in range(0, cx, 2):
            h = jnp.concatenate([src[j, x], src[j, x + 1]], axis=1)
            z_pair([h, h], band[:, 0:2 * cz], to, x)

    def x_column(i, carry):
        c = order(i)

        @pl.when(has_xl)
        def _():
            x_up(c).wait_recv()

        @pl.when(has_xh)
        def _():
            x_down(c).wait_recv()

        @pl.when(i + AHEAD < cy)
        def _():
            start_x(i + AHEAD, 0)

        def tile(z, c2):
            rows = pl.ds(pl.multiple_of(z * ZT, ZT), ZT)
            items = [xlo[c, k, rows, :].astype(F32) for k in range(RAD)]
            items += [movie[k, c, rows, :].astype(F32) for k in range(cx)]
            items += [xhi[c, k, rows, :].astype(F32) for k in range(RAD)]
            for x in range(cx):
                v = blur9(items, x)
                yb[x, rows, :] = v
                xsend[c, x, rows, :] = v.astype(BF16)
            return c2

        lax.fori_loop(0, cz // ZT, tile, 0)

        @pl.when(jnp.logical_and(i % 2 == 0, has_yl))
        def _():
            y_down(i // 2).start()

        @pl.when(jnp.logical_and(i % 2 == 1, has_yh))
        def _():
            y_up(RAD - 1 - i // 2).start()

        lanes = lax.broadcasted_iota(jnp.int32, (cx * cy, fr), 0)
        for x in range(0, cx, 2):
            parts = [split(yb[x + k]) for k in range(2)]
            hi = jnp.concatenate([p[0] for p in parts], axis=1)
            lo = jnp.concatenate([p[1] for p in parts], axis=1)
            z_pair([hi, hi, lo], band[...], c + RAD, x)
            for k in range(2):
                one = jnp.where(lanes == (x + k) * cy + c, 1.0, 0.0).astype(BF16)
                maskx[c, x + k] = jnp.dot(maskt[...], one, preferred_element_type=F32).astype(BF16)
        return carry

    lax.fori_loop(0, cy, x_column, 0)

    def save(c):
        return pltpu.make_async_copy(filt.at[c], filt_hbm.at[c], fsem.at[c])

    def y_column(c):
        def tile(z, carry):
            rows = pl.ds(pl.multiple_of(z * ZT, ZT), ZT)
            for x in range(cx):
                blur = blur9([zy[c + k, x, rows, :] for k in range(2 * RAD + 1)], 0)
                f = maskx[c, x, rows, :].astype(F32) * (movie[x, c, rows, :].astype(F32) - blur)
                fh, fl = split(f)
                filt[c, x, rows, 0:fr] = fh
                filt[c, x, rows, fr:2 * fr] = fl
            return carry
        lax.fori_loop(0, cz // ZT, tile, 0)
        save(c).start()
        both = filt[c].reshape(cx * cz, 2 * fr)
        gacc[...] += lax.dot_general(
            both[:, 0:fr], both, (((0,), (0,)), ((), ())), preferred_element_type=F32)

    def y_step(j, carry):
        @pl.when(has_yl)
        def _():
            y_up(RAD - 1 - j).wait_recv()

        @pl.when(has_yh)
        def _():
            y_down(j).wait_recv()
        halo_column(ylo, RAD - 1 - j, RAD - 1 - j)
        halo_column(yhi, j, cy + RAD + j)

        def two(s, c2):
            y_column(jnp.where(s == 0, RAD - 1 - j, cy - RAD + j))
            return c2
        lax.fori_loop(0, 2, two, 0)
        return carry

    lax.fori_loop(0, RAD, y_step, 0)

    g = gacc[:, 0:fr] + gacc[:, fr:2 * fr] + jnp.transpose(gacc[:, fr:2 * fr])
    r = fr // ny
    for p in range(ny):
        gpart[p] = g[p * r:(p + 1) * r]

    def scatter(d):
        to = lax.rem(gy + d, ny)
        return pltpu.make_async_remote_copy(
            src_ref=gpart.at[to], dst_ref=rsbuf.at[d], send_sem=s1.at[d], recv_sem=r1.at[d],
            device_id=(gx, to), device_id_type=MESH)

    def across(d):
        return pltpu.make_async_remote_copy(
            src_ref=xbuf.at[gx], dst_ref=xbuf.at[gx], send_sem=s2.at[d], recv_sem=r2.at[d],
            device_id=(lax.rem(gx + d, nx), gy), device_id_type=MESH)

    def gather(d):
        return pltpu.make_async_remote_copy(
            src_ref=gfull.at[gy], dst_ref=gfull.at[gy], send_sem=s3.at[d], recv_sem=r3.at[d],
            device_id=(gx, lax.rem(gy + d, ny)), device_id_type=MESH)

    def each(n, f):
        def body(d, c):
            f(d)
            return c
        lax.fori_loop(1, n, body, 0)

    each(ny, lambda d: scatter(d).start())
    each(ny, lambda d: scatter(d).wait_recv())
    total = gpart[gy]
    for d in range(1, ny):
        total = total + rsbuf[d]
    xbuf[gx] = total
    each(nx, lambda d: across(d).start())
    each(nx, lambda d: across(d).wait_recv())
    total = xbuf[0]
    for d in range(1, nx):
        total = total + xbuf[d]
    gfull[gy] = total
    each(ny, lambda d: gather(d).start())
    each(ny, lambda d: gather(d).wait_recv())
    gram_out[...] = gfull[...]

    each(ny, lambda d: scatter(d).wait_send())
    each(nx, lambda d: across(d).wait_send())
    each(ny, lambda d: gather(d).wait_send())

    def drain_x(c, carry):
        @pl.when(has_xh)
        def _():
            x_up(c).wait_send()

        @pl.when(has_xl)
        def _():
            x_down(c).wait_send()
        return carry

    def drain_y(j, carry):
        @pl.when(has_yh)
        def _():
            y_up(j).wait_send()

        @pl.when(has_yl)
        def _():
            y_down(j).wait_send()
        return carry

    def drain_f(c, carry):
        save(c).wait()
        return carry

    lax.fori_loop(0, cy, drain_f, 0)
    lax.fori_loop(0, cy, drain_x, 0)
    lax.fori_loop(0, RAD, drain_y, 0)


BLK = 8


def pieces(v):
    hi = v.astype(BF16)
    rest = v - hi.astype(F32)
    mid = rest.astype(BF16)
    return hi, mid, (rest - mid.astype(F32)).astype(BF16)


def outer(u, v):
    uh, um, ul = pieces(u)
    vh, vm, vl = pieces(v)
    left = jnp.concatenate([uh, uh, um, uh, ul, um], axis=0)
    right = jnp.concatenate([vh, vm, vh, vl, vh, vm], axis=0)
    return lax.dot_general(left, right, (((0,), (0,)), ((), ())), preferred_element_type=F32)


def stack(rows, sub):
    full = rows[0]
    for i in range(1, BLK):
        full = jnp.where(sub == i, rows[i], full)
    return full


def sweep(a, dbuf, zbuf):
    n = a.shape[0]
    cols = lax.broadcasted_iota(jnp.int32, (n, n), 1)
    lane = lax.broadcasted_iota(jnp.int32, (BLK, n), 1)
    sub = lax.broadcasted_iota(jnp.int32, (BLK, n), 0)
    panel = a[0:BLK, :]
    for start in range(0, n, BLK):
        after = start + BLK
        inside = (lane >= start) & (lane < after)
        u = jnp.where(inside, 0.0, panel)
        zbuf[start // BLK % 2] = jnp.where(lane == start + sub, -1.0, u)
        slot = start // BLK % 2
        for j in range(BLK):
            dbuf[slot, j] = jnp.broadcast_to(panel[:, start + j:start + j + 1], (BLK, n))
        if after < n:
            for j in range(BLK):
                dbuf[slot, BLK + j] = jnp.broadcast_to(panel[:, after + j:after + j + 1], (BLK, n))

        def entry(i, j):
            return jnp.broadcast_to(dbuf[slot, j, i:i + 1, :], (BLK, n))

        d = {(i, j): entry(i, j) for j in range(BLK) for i in range(j + 1)}
        z = [jnp.broadcast_to(zbuf[slot, i:i + 1, :], (BLK, n)) for i in range(BLK)]
        inverses, multipliers = {}, {}
        for s in range(0, BLK, 2):
            p, q, r = d[s, s], d[s, s + 1], d[s + 1, s + 1]
            inv = 1.0 / (p * r - q * q)
            ip, iq, ir = r * inv, -(q * inv), p * inv
            inverses[s] = (ip, iq, ir)
            for i in range(s + 2, BLK):
                m0 = d[s, i] * ip + d[s + 1, i] * iq
                m1 = d[s, i] * iq + d[s + 1, i] * ir
                multipliers[s, i] = (m0, m1)
                for j in range(i, BLK):
                    d[i, j] = d[i, j] - (m0 * d[s, j] + m1 * d[s + 1, j])
                z[i] = z[i] - (m0 * z[s] + m1 * z[s + 1])
        for s in range(BLK - 2, -1, -2):
            ip, iq, ir = inverses[s]
            w0, w1 = ip * z[s] + iq * z[s + 1], iq * z[s] + ir * z[s + 1]
            for i in range(BLK - 1, s + 1, -1):
                m0, m1 = multipliers[s, i]
                w0, w1 = w0 - m0 * z[i], w1 - m1 * z[i]
            z[s], z[s + 1] = w0, w1
        if after < n:
            rows = []
            for i in range(BLK):
                terms = [entry(s, BLK + i) * z[s] for s in range(BLK)]
                while len(terms) > 1:
                    terms = [terms[k] + terms[k + 1] for k in range(0, len(terms), 2)]
                rows.append(terms[0])
            panel = jnp.where(inside, 0.0, a[after:after + BLK, :]) - stack(rows, sub)
        full = stack(z, sub)
        a[...] = jnp.where((cols >= start) & (cols < after), 0.0, a[...]) - outer(u, full)
        a[start:after, :] = full


def fit_kernel(gram, filt_hbm, out_hbm, prop, a, m, dbuf, zbuf, filt, out, isem, osem):
    fr = gram.shape[0]
    load = pltpu.make_async_copy(filt_hbm, filt, isem.at[0])
    load.start()

    g = gram[...]
    row = lax.broadcasted_iota(jnp.int32, (fr, fr), 0)
    col = lax.broadcasted_iota(jnp.int32, (fr, fr), 1)
    diag = jnp.where((row == col) & (row < fr - 1), g, 0.0)
    lam = 0.5 * jnp.sum(diag) / (fr - 1)
    scaled = g / lam
    last = (row == fr - 1) | (col == fr - 1)
    a[...] = jnp.where(last, 0.0, scaled) + jnp.where(row == col, 1.0, 0.0)
    sweep(a, dbuf, zbuf)
    x = -jnp.dot(a[...], jnp.where(row == fr - 1, 0.0, scaled),
                 precision=lax.Precision.HIGHEST, preferred_element_type=F32)
    prop[...] = x[0:fr - 1, 1:fr]
    adv = jnp.where(col == 0, jnp.where(row == 0, 1.0, 0.0), x)
    mh, ml = split(adv)
    m[0:fr, 0:fr] = mh
    m[0:fr, fr:2 * fr] = ml
    m[fr:2 * fr, 0:fr] = mh
    m[fr:2 * fr, fr:2 * fr] = jnp.zeros((fr, fr), BF16)

    load.wait()

    def save(i):
        return pltpu.make_async_copy(out.at[i], out_hbm.at[i], osem.at[i])

    def layer(i, c):
        for y in range(out.shape[1]):
            v = jnp.dot(filt[y, i], m[...], preferred_element_type=F32)
            out[i, y] = (v[:, 0:fr] + v[:, fr:2 * fr]).astype(BF16)
        save(i).start()
        return c

    def drain(i, c):
        save(i).wait()
        return c

    lax.fori_loop(0, out.shape[0], layer, 0)
    lax.fori_loop(0, out.shape[0], drain, 0)


def on_device(nx, ny, movie, brain_mask):
    cx, cy, cz, fr = movie.shape
    r = fr // ny
    vmem = pl.BlockSpec(memory_space=pltpu.VMEM)
    hbm = pl.BlockSpec(memory_space=pltpu.HBM)
    dma = pltpu.SemaphoreType.DMA
    filt, gram = pl.pallas_call(
        functools.partial(filter_kernel, nx, ny),
        out_shape=(
            jax.ShapeDtypeStruct((cy, cx, cz, 2 * fr), BF16),
            jax.ShapeDtypeStruct((ny, r, fr), F32),
        ),
        in_specs=[hbm, hbm],
        out_specs=(hbm, vmem),
        scratch_shapes=[
            pltpu.VMEM((cx, cy, cz, fr), BF16),
            pltpu.VMEM((cx, cy, cz), jnp.int32),
            dma((2,)),
            pltpu.VMEM((cy, cx, cz, 2 * fr), BF16),
            dma((cy,)),
            pltpu.VMEM((cy, RAD, cz, fr), BF16),
            pltpu.VMEM((cy, RAD, cz, fr), BF16),
            pltpu.VMEM((cy, cx, cz, fr), BF16),
            pltpu.VMEM((RAD, cx, cz, fr), BF16),
            pltpu.VMEM((RAD, cx, cz, fr), BF16),
            pltpu.VMEM((cy + 2 * RAD, cx, cz, fr), F32),
            pltpu.VMEM((cx, cz, fr), F32),
            pltpu.VMEM((cy, cx, cz, fr), BF16),
            pltpu.VMEM((cz, 3 * cz), BF16),
            pltpu.VMEM((cz, cx * cy), BF16),
            pltpu.VMEM((fr, 2 * fr), F32),
            pltpu.VMEM((ny, r, fr), F32),
            pltpu.VMEM((ny, r, fr), F32),
            pltpu.VMEM((nx, r, fr), F32),
            pltpu.VMEM((ny, r, fr), F32),
            dma((cy,)), dma((cy,)), dma((cy,)), dma((cy,)),
            dma((RAD,)), dma((RAD,)), dma((RAD,)), dma((RAD,)),
            dma((ny,)), dma((ny,)), dma((nx,)), dma((nx,)), dma((ny,)), dma((ny,)),
        ],
        compiler_params=pltpu.CompilerParams(
            collective_id=0, has_side_effects=True, vmem_limit_bytes=60 * 1024 * 1024),
    )(movie, brain_mask)
    gram = gram.reshape(fr, fr)
    fitted, propagator = pl.pallas_call(
        fit_kernel,
        out_shape=(
            jax.ShapeDtypeStruct((cx, cy, cz, fr), BF16),
            jax.ShapeDtypeStruct((fr - 1, fr - 1), F32),
        ),
        in_specs=[vmem, hbm],
        out_specs=(hbm, vmem),
        scratch_shapes=[
            pltpu.VMEM((fr, fr), F32),
            pltpu.VMEM((2 * fr, 2 * fr), BF16),
            pltpu.VMEM((2, 2 * BLK, BLK, fr), F32),
            pltpu.VMEM((2, BLK, fr), F32),
            pltpu.VMEM((cy, cx, cz, 2 * fr), BF16),
            pltpu.VMEM((cx, cy, cz, fr), BF16),
            dma((1,)),
            dma((cx,)),
        ],
        compiler_params=pltpu.CompilerParams(vmem_limit_bytes=60 * 1024 * 1024),
    )(gram, filt)
    return fitted, propagator


def solution(mesh):
    nx, ny = mesh.shape["gx"], mesh.shape["gy"]
    return jax.shard_map(
        functools.partial(on_device, nx, ny),
        mesh=mesh,
        in_specs=(P("gx", "gy", None, None), P("gx", "gy", None)),
        out_specs=(P("gx", "gy", None, None), P()),
        check_vma=False,
    )
```

time: 61.2 us -> 58.6 us (0.958)
  Pallas kernels: 60.4 us -> 57.8 us
    pallas_call x1, Pallas kernels: 11.1 us -> 8.19 us  [on_device(): pl.pallas_call(fit_kernel, out_shape=(jax.ShapeDtypeStruct((cx, cy, cz, f...]
where the time goes in v4:
time: 58.6 us; the launch traced here: 58.4 us
  Pallas kernels  57.8 us (99%)
  between operations  0.64 us (1%)
    pallas_call x1, Pallas kernels, on_device(): pl.pallas_call(functools.partial(filter_kernel, nx, ny), out_shape=(jax.S...  49.6 us
    pallas_call x1, Pallas kernels, on_device(): pl.pallas_call(fit_kernel, out_shape=(jax.ShapeDtypeStruct((cx, cy, cz, f...  8.19 us

profile of v4, /device:TPU:0, one launch (start us, length us, event | category | flops | bytes accessed | tf_op | source)
XLA Modules:
  0.0 58.4 jit_solution(1715847229066949741)
XLA Ops:
  0.6 49.6 %shard_map.41 = (bf16[8,8,128,256]{3,2,1,0:T(8,128)(2,1)}, f32[8,16,128]{2,1,0:T(8,128)}) custom-call(bf16[8,8,128,128]{3,2,1,0:T(8,128)(2,1)} %movie_hbm.1, s32[8,8,128]{2,1,0:T(8,128)} %mask_hbm.1), custom_call_target="tpu_custom_call" | custom-call | tf_op jit(solution)/shard_map/pallas_call | solution.py:446
  50.2 8.2 %shard_map.42 = (bf16[8,8,128,128]{3,2,1,0:T(8,128)(2,1)}, f32[127,127]{1,0:T(8,128)}) custom-call(f32[128,128]{1,0:T(8,128)} %bitcast.1, bf16[8,8,128,256]{3,2,1,0:T(8,128)(2,1)} %get-tuple-element.5.filt_hbm), custom_call_target="tpu_custom_call" | custom-call | tf_op jit(solution)/shard_map/pallas_call | solution.py:483

commit v5 on v4

--- a/solution.py
+++ b/solution.py
@@ -149,6 +149,19 @@
             h = jnp.concatenate([src[j, x], src[j, x + 1]], axis=1)
             z_pair([h, h], band[:, 0:2 * cz], to, x)
 
+    def take_halo(j):
+        @pl.when(has_yl)
+        def _():
+            y_up(RAD - 1 - j).wait_recv()
+
+        @pl.when(has_yh)
+        def _():
+            y_down(j).wait_recv()
+        halo_column(ylo, RAD - 1 - j, RAD - 1 - j)
+        halo_column(yhi, j, cy + RAD + j)
+
+    early = 2
+
     def x_column(i, carry):
         c = order(i)
 
@@ -194,6 +207,10 @@
             for k in range(2):
                 one = jnp.where(lanes == (x + k) * cy + c, 1.0, 0.0).astype(BF16)
                 maskx[c, x + k] = jnp.dot(maskt[...], one, preferred_element_type=F32).astype(BF16)
+
+        @pl.when(jnp.logical_and(i >= 5, i < 5 + early))
+        def _():
+            take_halo(i - 5)
         return carry
 
     lax.fori_loop(0, cy, x_column, 0)
@@ -218,15 +235,9 @@
             both[:, 0:fr], both, (((0,), (0,)), ((), ())), preferred_element_type=F32)
 
     def y_step(j, carry):
-        @pl.when(has_yl)
-        def _():
-            y_up(RAD - 1 - j).wait_recv()
-
-        @pl.when(has_yh)
-        def _():
-            y_down(j).wait_recv()
-        halo_column(ylo, RAD - 1 - j, RAD - 1 - j)
-        halo_column(yhi, j, cy + RAD + j)
+        @pl.when(j >= early)
+        def _():
+            take_halo(j)
 
         def two(s, c2):
             y_column(jnp.where(s == 0, RAD - 1 - j, cy - RAD + j))

time: 58.6 us -> 58.5 us (level)
  no operation moved by 1% of the time
where the time goes in v5:
time: 58.5 us; the launch traced here: 58.4 us
  Pallas kernels  57.7 us (99%)
  between operations  0.64 us (1%)
    pallas_call x1, Pallas kernels, on_device(): pl.pallas_call(functools.partial(filter_kernel, nx, ny), out_shape=(jax.S...  49.5 us
    pallas_call x1, Pallas kernels, on_device(): pl.pallas_call(fit_kernel, out_shape=(jax.ShapeDtypeStruct((cx, cy, cz, f...  8.19 us

profile of v5, /device:TPU:0, one launch (start us, length us, event | category | flops | bytes accessed | tf_op | source)
XLA Modules:
  0.0 58.4 jit_solution(12216060992547412058)
XLA Ops:
  0.6 49.5 %shard_map.41 = (bf16[8,8,128,256]{3,2,1,0:T(8,128)(2,1)}, f32[8,16,128]{2,1,0:T(8,128)}) custom-call(bf16[8,8,128,128]{3,2,1,0:T(8,128)(2,1)} %movie_hbm.1, s32[8,8,128]{2,1,0:T(8,128)} %mask_hbm.1), custom_call_target="tpu_custom_call" | custom-call | tf_op jit(solution)/shard_map/pallas_call | solution.py:457
  50.2 8.2 %shard_map.42 = (bf16[8,8,128,128]{3,2,1,0:T(8,128)(2,1)}, f32[127,127]{1,0:T(8,128)}) custom-call(f32[128,128]{1,0:T(8,128)} %bitcast.1, bf16[8,8,128,256]{3,2,1,0:T(8,128)(2,1)} %get-tuple-element.5.filt_hbm), custom_call_target="tpu_custom_call" | custom-call | tf_op jit(solution)/shard_map/pallas_call | solution.py:494

commit v6 on v4

--- a/solution.py
+++ b/solution.py
@@ -423,9 +423,9 @@
         return pltpu.make_async_copy(out.at[i], out_hbm.at[i], osem.at[i])
 
     def layer(i, c):
-        for y in range(out.shape[1]):
-            v = jnp.dot(filt[y, i], m[...], preferred_element_type=F32)
-            out[i, y] = (v[:, 0:fr] + v[:, fr:2 * fr]).astype(BF16)
+        rows = filt[:, i].reshape(-1, 2 * fr)
+        v = jnp.dot(rows, m[...], preferred_element_type=F32)
+        out[i] = (v[:, 0:fr] + v[:, fr:2 * fr]).astype(BF16).reshape(out.shape[1:])
         save(i).start()
         return c
 

time: 58.6 us -> 58.4 us (level)
  no operation moved by 1% of the time
where the time goes in v6:
time: 58.4 us; the launch traced here: 58.3 us
  Pallas kernels  57.6 us (99%)
  between operations  0.64 us (1%)
    pallas_call x1, Pallas kernels, on_device(): pl.pallas_call(functools.partial(filter_kernel, nx, ny), out_shape=(jax.S...  49.6 us
    pallas_call x1, Pallas kernels, on_device(): pl.pallas_call(fit_kernel, out_shape=(jax.ShapeDtypeStruct((cx, cy, cz, f...  8.06 us

profile of v6, /device:TPU:0, one launch (start us, length us, event | category | flops | bytes accessed | tf_op | source)
XLA Modules:
  0.0 58.3 jit_solution(1493517253904891399)
XLA Ops:
  0.6 49.6 %shard_map.41 = (bf16[8,8,128,256]{3,2,1,0:T(8,128)(2,1)}, f32[8,16,128]{2,1,0:T(8,128)}) custom-call(bf16[8,8,128,128]{3,2,1,0:T(8,128)(2,1)} %movie_hbm.1, s32[8,8,128]{2,1,0:T(8,128)} %mask_hbm.1), custom_call_target="tpu_custom_call" | custom-call | tf_op jit(solution)/shard_map/pallas_call | solution.py:446
  50.2 8.1 %shard_map.42 = (bf16[8,8,128,128]{3,2,1,0:T(8,128)(2,1)}, f32[127,127]{1,0:T(8,128)}) custom-call(f32[128,128]{1,0:T(8,128)} %bitcast.1, bf16[8,8,128,256]{3,2,1,0:T(8,128)(2,1)} %get-tuple-element.5.filt_hbm), custom_call_target="tpu_custom_call" | custom-call | tf_op jit(solution)/shard_map/pallas_call | solution.py:483

commit v7 on v6

--- a/solution.py
+++ b/solution.py
@@ -9,7 +9,7 @@
 from jax.sharding import PartitionSpec as P
 
 RAD = 4
-AHEAD = 3
+AHEAD = 5
 MESH = pl.DeviceIdType.MESH
 F32 = jnp.float32
 BF16 = jnp.bfloat16

time: 58.4 us -> 58.4 us (level)
  no operation moved by 1% of the time
where the time goes in v7:
time: 58.4 us; the launch traced here: 58.3 us
  Pallas kernels  57.6 us (99%)
  between operations  0.64 us (1%)
    pallas_call x1, Pallas kernels, on_device(): pl.pallas_call(functools.partial(filter_kernel, nx, ny), out_shape=(jax.S...  49.6 us
    pallas_call x1, Pallas kernels, on_device(): pl.pallas_call(fit_kernel, out_shape=(jax.ShapeDtypeStruct((cx, cy, cz, f...  8.06 us

profile of v7, /device:TPU:0, one launch (start us, length us, event | category | flops | bytes accessed | tf_op | source)
XLA Modules:
  0.0 58.3 jit_solution(10019614415815000964)
XLA Ops:
  0.6 49.6 %shard_map.41 = (bf16[8,8,128,256]{3,2,1,0:T(8,128)(2,1)}, f32[8,16,128]{2,1,0:T(8,128)}) custom-call(bf16[8,8,128,128]{3,2,1,0:T(8,128)(2,1)} %movie_hbm.1, s32[8,8,128]{2,1,0:T(8,128)} %mask_hbm.1), custom_call_target="tpu_custom_call" | custom-call | tf_op jit(solution)/shard_map/pallas_call | solution.py:446
  50.2 8.1 %shard_map.42 = (bf16[8,8,128,128]{3,2,1,0:T(8,128)(2,1)}, f32[127,127]{1,0:T(8,128)}) custom-call(f32[128,128]{1,0:T(8,128)} %bitcast.1, bf16[8,8,128,256]{3,2,1,0:T(8,128)(2,1)} %get-tuple-element.5.filt_hbm), custom_call_target="tpu_custom_call" | custom-call | tf_op jit(solution)/shard_map/pallas_call | solution.py:483
